TPU v7x, 32 devices: a whole 2x2x4 slice. The times are simulated.
32 devices in a mesh: lines: 2 (over y), strip: 8 (over z, x), wave: 2 (over core).
Axes of the slice: x: 2, y: 2, z: 4, core: 2. Of those that a mesh axis runs over, the one named last changes fastest.
Arguments:
- prior_fields: float32 [12, 2, 128, 2048], P('wave', None, ('lines', 'strip')), parts along dimension 2, may hold values from -4 to 4
- conductivity: float32 [128, 2048], P(('lines', 'strip')), parts along dimension 0, may hold values from 0.2 to 5
- electrode_nodes: int32 [128], P('lines'), parts along dimension 0, may hold values from 0 to 131071, as said below
- source_pair: int32 [4], P('lines'), parts along dimension 0, may hold values from 0 to 63
- innovation: float32 [128], P('lines'), parts along dimension 0, may hold values from -6 to 6
Outputs:
- gradient: float32 [128, 2048], P(('lines', 'strip'), 'wave'), parts along dimension 0
There are 2 independent parts, one for each index of `lines`. A program takes and returns all parts, laid end to end along the dimension named above; each array names one. Nothing has to cross between parts.
Inputs may be any that keep to these rules, and one draw needn't show every extreme that they name: `electrode_nodes`: nodes may repeat. `source_pair`: the two numbers may be equal.
All inputs are finite; a program needn't handle non-finite values.
Results may differ from a plain program's by a relative error of at most 0.0003.
Values sent between devices are 32-bit elements; how exact they have to be, the bound alone decides.
A program may use at most 64 MiB of HBM per device.

v0:
```python
import math

import jax
import jax.numpy as jnp
from jax import lax
from jax.sharding import PartitionSpec as P

WAVES = 12
ITERS = 12


k_lowest = 0.01
k_highest = 1.0


def padded_2(block, sides, width):
    for axis, dim in sides:
        count = lax.axis_size(axis)
        forward = [(i, i + 1) for i in range(count - 1)]
        backward = [(target, source) for source, target in forward]
        low = lax.ppermute(
            lax.slice_in_dim(block, block.shape[dim] - width, None, axis=dim), axis, forward
        )
        high = lax.ppermute(lax.slice_in_dim(block, 0, width, axis=dim), axis, backward)
        block = jnp.concatenate([low, block, high], axis=dim)
    return block


def wave_table(position):
    spacing = (math.log(k_highest) - math.log(k_lowest)) / (WAVES - 1)
    wavenum = jnp.exp(math.log(k_lowest) + spacing * position)
    ends = jnp.where((position == 0) | (position == WAVES - 1), 0.5, 1.0)
    weights = 2.0 / math.pi * spacing * wavenum * ends
    return (wavenum, weights)


def inner_sums(first, second):
    return jnp.sum(first * second, axis=(2, 3), keepdims=True)


def per_device(prior_fields, conductivity, electrode_nodes, source_pair, innovation):
    wave_dev = prior_fields.shape[0]
    row_count = prior_fields.shape[2]
    cell_count = prior_fields.shape[3]
    row_ids = lax.axis_index("strip") * row_count + jnp.arange(row_count, dtype=jnp.int32)
    top_keep = (row_ids != 0)[:, None]
    sig_pad = padded_2(conductivity, (("strip", 0),), 1)
    sig_pad = jnp.pad(sig_pad, ((0, 0), (1, 1)))
    face_up = jnp.where(top_keep, 0.5 * (conductivity + sig_pad[:-2, 1:-1]), 0.0)
    face_down = 0.5 * (conductivity + sig_pad[2:, 1:-1])
    face_left = 0.5 * (conductivity + sig_pad[1:-1, :-2])
    face_right = 0.5 * (conductivity + sig_pad[1:-1, 2:])
    wave_ids = (lax.axis_index("wave") * wave_dev + jnp.arange(wave_dev, dtype=jnp.int32)).astype(
        jnp.float32
    )
    wavenum, weights = wave_table(wave_ids)
    face_sum = face_up + face_down + face_left + face_right
    diagonal = (face_sum[None] + (wavenum * wavenum)[:, None, None] * conductivity[None])[:, None]

    def operate(vector):
        padded = padded_2(vector, (("strip", 2),), 1)
        padded = jnp.pad(padded, ((0, 0), (0, 0), (0, 0), (1, 1)))
        result = diagonal * vector - face_up * padded[:, :, :-2, 1:-1]
        result = result - face_down * padded[:, :, 2:, 1:-1]
        result = result - face_left * padded[:, :, 1:-1, :-2]
        return result - face_right * padded[:, :, 1:-1, 2:]

    electrode_ids = jnp.arange(innovation.shape[0], dtype=jnp.int32)
    forward = (electrode_ids == source_pair[0]).astype(jnp.float32) - (
        electrode_ids == source_pair[1]
    ).astype(jnp.float32)
    values = jnp.stack([forward, innovation])
    node_rows = electrode_nodes // cell_count
    node_cols = electrode_nodes % cell_count
    rows_hot = (node_rows[:, None] == row_ids[None, :]).astype(jnp.float32)
    cols_hot = (node_cols[:, None] == jnp.arange(cell_count, dtype=jnp.int32)[None, :]).astype(
        jnp.float32
    )
    weighted = values[:, :, None] * rows_hot[None]
    source = jnp.einsum("sez,ex->szx", weighted, cols_hot, precision=lax.Precision.HIGHEST)[None]
    solution = prior_fields
    residual = source - operate(solution)

    def both_sums(vector, applied):
        return lax.psum((inner_sums(vector, vector), inner_sums(vector, applied)), "strip")

    applied = operate(residual)
    norm_now, product = both_sums(residual, applied)
    step_size = norm_now / product

    def iterate(sweep, carry):
        solution, residual, direction, along_dir, norm_now, step_size = carry
        solution = solution + step_size * direction
        residual = residual - step_size * along_dir
        applied = operate(residual)
        norm_next, product = both_sums(residual, applied)
        beta_ratio = norm_next / norm_now
        step_next = norm_next / (product - beta_ratio * norm_next / step_size)
        direction = residual + beta_ratio * direction
        along_dir = applied + beta_ratio * along_dir
        return (solution, residual, direction, along_dir, norm_next, step_next)

    carry = (solution, residual, residual, applied, norm_now, step_size)
    solution, residual, direction, along_dir, norm_now, step_size = lax.fori_loop(
        0, ITERS - 1, iterate, carry
    )
    solution = solution + step_size * direction
    sol_pad = padded_2(solution, (("strip", 2),), 1)
    sol_pad = jnp.pad(sol_pad, ((0, 0), (0, 0), (0, 0), (1, 1)))
    forward_field = solution[:, 0]
    adjoint_field = solution[:, 1]
    fwd_pad = sol_pad[:, 0]
    adj_pad = sol_pad[:, 1]
    term_up = jnp.where(
        top_keep[None],
        (forward_field - fwd_pad[:, :-2, 1:-1]) * (adjoint_field - adj_pad[:, :-2, 1:-1]),
        0.0,
    )
    term_down = (forward_field - fwd_pad[:, 2:, 1:-1]) * (adjoint_field - adj_pad[:, 2:, 1:-1])
    term_left = (forward_field - fwd_pad[:, 1:-1, :-2]) * (adjoint_field - adj_pad[:, 1:-1, :-2])
    term_right = (forward_field - fwd_pad[:, 1:-1, 2:]) * (adjoint_field - adj_pad[:, 1:-1, 2:])
    partial_value = (wavenum * wavenum)[:, None, None] * forward_field * adjoint_field + 0.5 * (
        term_up + term_down + term_left + term_right
    )
    local_sum = jnp.sum(weights[:, None, None] * partial_value, axis=0)
    summed = lax.psum(local_sum, "wave")
    share_width = cell_count // lax.axis_size("wave")
    share_out = lax.dynamic_slice_in_dim(
        summed, lax.axis_index("wave") * share_width, share_width, 1
    )
    return -share_out


def solution(mesh):
    in_specs = (
        P("wave", None, ("lines", "strip"), None),
        P(("lines", "strip"), None),
        P("lines"),
        P("lines"),
        P("lines"),
    )
    out_specs = P(("lines", "strip"), "wave")
    return jax.shard_map(
        per_device, mesh=mesh, in_specs=in_specs, out_specs=out_specs, check_vma=False
    )
```

profile of v0, /device:TPU:1, one launch (start us, length us, event | category | flops | bytes accessed | tf_op | source)
XLA Modules:
  0.0 484.3 jit_solution(14914242999981153592)
XLA Ops:
  9.9 4.6 collective-permute-start.2
  14.7 4.3 collective-permute-start.4
  29.1 4.0 collective-permute-start.6
  35.3 3.1 collective-permute-done.7
  41.4 16.6 %all-reduce.6 = (f32[6,2,1,1]{0,1,3,2:T(2,128)}, f32[6,2,1,1]{0,1,3,2:T(2,128)S(1)}) all-reduce(f32[6,2,1,1]{0,1,3,2:T(2,128)S(1)} %bitcast.49, f32[6,2,1,1]{0,1,3,2:T(2,128)S(1)} %bitcast.48), channel_id=1, replica_groups=mesh['lines'=2,'strip'=8,'wave'=2] {'strip'}, use_global_device_ids=true, to_apply=%region_1.2 | all-reduce | flops 24 | bytes 192 | tf_op jit(solution)/shard_map/psum | solution.py:85
  58.7 326.2 %while.23 = (s32[]{:T(128)}, f32[6,2,8,2048]{3,2,1,0:T(8,128)S(1)}, f32[6,2,8,2048]{3,2,1,0:T(8,128)S(1)}, f32[6,2,8,2048]{3,2,1,0:T(8,128)}, f32[6,2,8,2048]{3,...) while((s32[]{:T(128)}, f32[6,2,8,2048]{3,2,1,0:T(8,128)S(1)}, ...), condition=%wide.region_9.10_spmd.clone, body=%wide.region_4.9_spmd.clone.sunk | while | flops 6686654 | bytes 17107604 | solution.py:104
  60.4 4.0 collective-permute-start.1
  69.1 15.5 %all-reduce.8 = (f32[6,2,1,1]{0,1,3,2:T(2,128)S(1)}, f32[6,2,1,1]{0,1,3,2:T(2,128)S(1)}) all-reduce(f32[6,2,1,1]{0,1,3,2:T(2,128)S(1)} %bitcast.45, f32[6,2,1,1]{0,1,3,2:T(2,128)S(1)} %bitcast.46), channel_id=1, replica_groups=mesh['lines'=2,'strip'=8,'wave'=2] {'strip'}, use_global_device_ids=true, to_apply=%region_6.6 | all-reduce | flops 24 | bytes 192 | tf_op jit(solution)/shard_map/while/body/eval_jaxpr/psum | solution.py:85
  85.9 2.3 multiply_add_fusion.6
  89.9 4.0 collective-permute-start.1
  98.6 15.5 %all-reduce.8 = (f32[6,2,1,1]{0,1,3,2:T(2,128)S(1)}, f32[6,2,1,1]{0,1,3,2:T(2,128)S(1)}) all-reduce(f32[6,2,1,1]{0,1,3,2:T(2,128)S(1)} %bitcast.45, f32[6,2,1,1]{0,1,3,2:T(2,128)S(1)} %bitcast.46), channel_id=1, replica_groups=mesh['lines'=2,'strip'=8,'wave'=2] {'strip'}, use_global_device_ids=true, to_apply=%region_6.6 | all-reduce | flops 24 | bytes 192 | tf_op jit(solution)/shard_map/while/body/eval_jaxpr/psum | solution.py:85
  119.4 4.0 collective-permute-start.1
  128.1 15.6 %all-reduce.8 = (f32[6,2,1,1]{0,1,3,2:T(2,128)S(1)}, f32[6,2,1,1]{0,1,3,2:T(2,128)S(1)}) all-reduce(f32[6,2,1,1]{0,1,3,2:T(2,128)S(1)} %bitcast.45, f32[6,2,1,1]{0,1,3,2:T(2,128)S(1)} %bitcast.46), channel_id=1, replica_groups=mesh['lines'=2,'strip'=8,'wave'=2] {'strip'}, use_global_device_ids=true, to_apply=%region_6.6 | all-reduce | flops 24 | bytes 192 | tf_op jit(solution)/shard_map/while/body/eval_jaxpr/psum | solution.py:85
  149.0 4.0 collective-permute-start.1
  157.7 15.5 %all-reduce.8 = (f32[6,2,1,1]{0,1,3,2:T(2,128)S(1)}, f32[6,2,1,1]{0,1,3,2:T(2,128)S(1)}) all-reduce(f32[6,2,1,1]{0,1,3,2:T(2,128)S(1)} %bitcast.45, f32[6,2,1,1]{0,1,3,2:T(2,128)S(1)} %bitcast.46), channel_id=1, replica_groups=mesh['lines'=2,'strip'=8,'wave'=2] {'strip'}, use_global_device_ids=true, to_apply=%region_6.6 | all-reduce | flops 24 | bytes 192 | tf_op jit(solution)/shard_map/while/body/eval_jaxpr/psum | solution.py:85
  178.5 4.0 collective-permute-start.1
  187.2 15.7 %all-reduce.8 = (f32[6,2,1,1]{0,1,3,2:T(2,128)S(1)}, f32[6,2,1,1]{0,1,3,2:T(2,128)S(1)}) all-reduce(f32[6,2,1,1]{0,1,3,2:T(2,128)S(1)} %bitcast.45, f32[6,2,1,1]{0,1,3,2:T(2,128)S(1)} %bitcast.46), channel_id=1, replica_groups=mesh['lines'=2,'strip'=8,'wave'=2] {'strip'}, use_global_device_ids=true, to_apply=%region_6.6 | all-reduce | flops 24 | bytes 192 | tf_op jit(solution)/shard_map/while/body/eval_jaxpr/psum | solution.py:85
  208.2 4.0 collective-permute-start.1
  216.9 15.5 %all-reduce.8 = (f32[6,2,1,1]{0,1,3,2:T(2,128)S(1)}, f32[6,2,1,1]{0,1,3,2:T(2,128)S(1)}) all-reduce(f32[6,2,1,1]{0,1,3,2:T(2,128)S(1)} %bitcast.45, f32[6,2,1,1]{0,1,3,2:T(2,128)S(1)} %bitcast.46), channel_id=1, replica_groups=mesh['lines'=2,'strip'=8,'wave'=2] {'strip'}, use_global_device_ids=true, to_apply=%region_6.6 | all-reduce | flops 24 | bytes 192 | tf_op jit(solution)/shard_map/while/body/eval_jaxpr/psum | solution.py:85
  237.7 4.0 collective-permute-start.1
  247.4 15.5 %all-reduce.8 = (f32[6,2,1,1]{0,1,3,2:T(2,128)S(1)}, f32[6,2,1,1]{0,1,3,2:T(2,128)S(1)}) all-reduce(f32[6,2,1,1]{0,1,3,2:T(2,128)S(1)} %bitcast.45, f32[6,2,1,1]{0,1,3,2:T(2,128)S(1)} %bitcast.46), channel_id=1, replica_groups=mesh['lines'=2,'strip'=8,'wave'=2] {'strip'}, use_global_device_ids=true, to_apply=%region_6.6 | all-reduce | flops 24 | bytes 192 | tf_op jit(solution)/shard_map/while/body/eval_jaxpr/psum | solution.py:85
  268.3 4.0 collective-permute-start.1
  277.0 15.5 %all-reduce.8 = (f32[6,2,1,1]{0,1,3,2:T(2,128)S(1)}, f32[6,2,1,1]{0,1,3,2:T(2,128)S(1)}) all-reduce(f32[6,2,1,1]{0,1,3,2:T(2,128)S(1)} %bitcast.45, f32[6,2,1,1]{0,1,3,2:T(2,128)S(1)} %bitcast.46), channel_id=1, replica_groups=mesh['lines'=2,'strip'=8,'wave'=2] {'strip'}, use_global_device_ids=true, to_apply=%region_6.6 | all-reduce | flops 24 | bytes 192 | tf_op jit(solution)/shard_map/while/body/eval_jaxpr/psum | solution.py:85
  293.8 2.3 multiply_add_fusion.6
  297.8 4.0 collective-permute-start.1
  306.5 15.5 %all-reduce.8 = (f32[6,2,1,1]{0,1,3,2:T(2,128)S(1)}, f32[6,2,1,1]{0,1,3,2:T(2,128)S(1)}) all-reduce(f32[6,2,1,1]{0,1,3,2:T(2,128)S(1)} %bitcast.45, f32[6,2,1,1]{0,1,3,2:T(2,128)S(1)} %bitcast.46), channel_id=1, replica_groups=mesh['lines'=2,'strip'=8,'wave'=2] {'strip'}, use_global_device_ids=true, to_apply=%region_6.6 | all-reduce | flops 24 | bytes 192 | tf_op jit(solution)/shard_map/while/body/eval_jaxpr/psum | solution.py:85
  327.3 4.0 collective-permute-start.1
  336.0 15.8 %all-reduce.8 = (f32[6,2,1,1]{0,1,3,2:T(2,128)S(1)}, f32[6,2,1,1]{0,1,3,2:T(2,128)S(1)}) all-reduce(f32[6,2,1,1]{0,1,3,2:T(2,128)S(1)} %bitcast.45, f32[6,2,1,1]{0,1,3,2:T(2,128)S(1)} %bitcast.46), channel_id=1, replica_groups=mesh['lines'=2,'strip'=8,'wave'=2] {'strip'}, use_global_device_ids=true, to_apply=%region_6.6 | all-reduce | flops 24 | bytes 192 | tf_op jit(solution)/shard_map/while/body/eval_jaxpr/psum | solution.py:85
  357.1 4.0 collective-permute-start.1
  365.8 15.5 %all-reduce.8 = (f32[6,2,1,1]{0,1,3,2:T(2,128)S(1)}, f32[6,2,1,1]{0,1,3,2:T(2,128)S(1)}) all-reduce(f32[6,2,1,1]{0,1,3,2:T(2,128)S(1)} %bitcast.45, f32[6,2,1,1]{0,1,3,2:T(2,128)S(1)} %bitcast.46), channel_id=1, replica_groups=mesh['lines'=2,'strip'=8,'wave'=2] {'strip'}, use_global_device_ids=true, to_apply=%region_6.6 | all-reduce | flops 24 | bytes 192 | tf_op jit(solution)/shard_map/while/body/eval_jaxpr/psum | solution.py:85
  389.6 3.7 collective-permute-done.9
  396.3 79.8 %all-reduce.11.cloned.1.call-done = f32[8,2048]{1,0:T(8,128)} async-done(((f32[8,2048]{1,0:T(8,128)}), f32[8,2048]{1,0:T(8,128)}) %all-reduce.11.cloned.1.call-update) | async-done | bytes 65552 | tf_op jit(solution)/shard_map/psum | solution.py:126
  (306 shorter events, 134.3 us)
Async XLA Ops:
  6.5 15.7 %copy-start.7 = (f32[64]{0:T(128)S(1)}, f32[64]{0:T(128)}, u32[]{:S(2)}) copy-start(f32[64]{0:T(128)} %param.11) | copy-start | bytes 772
  6.5 469.5 %all-reduce.11.cloned.1.call-start = ((), (), s32[]{:S(2)}) async-start(), calls=%async_computation | async-start | bytes 131072 | tf_op jit(solution)/shard_map/psum | solution.py:126
  8.6 14.0 %collective-permute-start.3 = (f32[1,2048]{1,0:T(1,128)S(1)}, f32[1,2048]{1,0:T(1,128)S(1)}, u32[]{:S(2)}, u32[]{:S(2)}) collective-permute-start(f32[1,2048]{1,0:T(1,128)S(1)} %get-tuple-element.250), channel_id=1, source_target_pairs={{2,0},{4,2},{6,4},{8,6},{10,8},{12,10},{14,12},{3,1},{5,3},{7,5},{... | collective-permute-start | bytes 24584 | tf_op jit(solution)/shard_map/ppermute | solution.py:24
  9.9 12.7 %collective-permute-start.2 = (f32[1,2048]{1,0:T(1,128)S(1)}, f32[1,2048]{1,0:T(1,128)S(1)}, u32[]{:S(2)}, u32[]{:S(2)}) collective-permute-start(f32[1,2048]{1,0:T(1,128)S(1)} %get-tuple-element.251), channel_id=1, source_target_pairs={{0,2},{2,4},{4,6},{6,8},{8,10},{10,12},{12,14},{1,3},{3,5},{5,7},{... | collective-permute-start | bytes 24584 | tf_op jit(solution)/shard_map/ppermute | solution.py:21
  14.7 11.7 %collective-permute-start.4 = (f32[6,2,1,2048]{3,2,1,0:T(1,128)S(1)}, f32[6,2,1,2048]{3,2,1,0:T(1,128)S(1)}, u32[]{:S(2)}, u32[]{:S(2)}) collective-permute-start(f32[6,2,1,2048]{3,2,1,0:T(1,128)S(1)} %get-tuple-element.248), channel_id=1, source_target_pairs={{0,2},{2,4},{4,6},{6,8},{8,10},{10,12},{12,14},{1,3},{3,5},{5,7},{... | collective-permute-start | bytes 294920 | tf_op jit(solution)/shard_map/ppermute | solution.py:21
  18.9 7.5 %collective-permute-start.5 = (f32[6,2,1,2048]{3,2,1,0:T(1,128)S(1)}, f32[6,2,1,2048]{3,2,1,0:T(1,128)S(1)}, u32[]{:S(2)}, u32[]{:S(2)}) collective-permute-start(f32[6,2,1,2048]{3,2,1,0:T(1,128)S(1)} %get-tuple-element.249), channel_id=1, source_target_pairs={{2,0},{4,2},{6,4},{8,6},{10,8},{12,10},{14,12},{3,1},{5,3},{7,5},{... | collective-permute-start | bytes 294920 | tf_op jit(solution)/shard_map/ppermute | solution.py:24
  29.1 6.2 %collective-permute-start.6 = (f32[6,2,1,2048]{3,2,1,0:T(1,128)S(1)}, f32[6,2,1,2048]{3,2,1,0:T(1,128)S(1)}, u32[]{:S(2)}, u32[]{:S(2)}) collective-permute-start(f32[6,2,1,2048]{3,2,1,0:T(1,128)S(1)} %get-tuple-element.246), channel_id=1, source_target_pairs={{0,2},{2,4},{4,6},{6,8},{8,10},{10,12},{12,14},{1,3},{3,5},{5,7},{... | collective-permute-start | bytes 294920 | tf_op jit(solution)/shard_map/ppermute | solution.py:21
  33.1 5.4 %collective-permute-start.7 = (f32[6,2,1,2048]{3,2,1,0:T(1,128)S(1)}, f32[6,2,1,2048]{3,2,1,0:T(1,128)S(1)}, u32[]{:S(2)}, u32[]{:S(2)}) collective-permute-start(f32[6,2,1,2048]{3,2,1,0:T(1,128)S(1)} %get-tuple-element.247), channel_id=1, source_target_pairs={{2,0},{4,2},{6,4},{8,6},{10,8},{12,10},{14,12},{3,1},{5,3},{7,5},{... | collective-permute-start | bytes 294920 | tf_op jit(solution)/shard_map/ppermute | solution.py:24
  59.1 6.3 %collective-permute-start = (f32[6,2,1,2048]{3,2,1,0:T(1,128)S(1)}, f32[6,2,1,2048]{3,2,1,0:T(1,128)S(1)}, u32[]{:S(2)}, u32[]{:S(2)}) collective-permute-start(f32[6,2,1,2048]{3,2,1,0:T(1,128)S(1)} %get-tuple-element.353), channel_id=1, source_target_pairs={{2,0},{4,2},{6,4},{8,6},{10,8},{12,10},{14,12},{3,1},{5,3},{7,5},{... | collective-permute-start | bytes 294920 | tf_op jit(solution)/shard_map/while/body/eval_jaxpr/ppermute | solution.py:24
  60.4 5.6 %collective-permute-start.1 = (f32[6,2,1,2048]{3,2,1,0:T(1,128)S(1)}, f32[6,2,1,2048]{3,2,1,0:T(1,128)S(1)}, u32[]{:S(2)}, u32[]{:S(2)}) collective-permute-start(f32[6,2,1,2048]{3,2,1,0:T(1,128)S(1)} %get-tuple-element.354), channel_id=1, source_target_pairs={{0,2},{2,4},{4,6},{6,8},{8,10},{10,12},{12,14},{1,3},{3,5},{5,7},{... | collective-permute-start | bytes 294920 | tf_op jit(solution)/shard_map/while/body/eval_jaxpr/ppermute | solution.py:21
  88.6 6.3 %collective-permute-start = (f32[6,2,1,2048]{3,2,1,0:T(1,128)S(1)}, f32[6,2,1,2048]{3,2,1,0:T(1,128)S(1)}, u32[]{:S(2)}, u32[]{:S(2)}) collective-permute-start(f32[6,2,1,2048]{3,2,1,0:T(1,128)S(1)} %get-tuple-element.353), channel_id=1, source_target_pairs={{2,0},{4,2},{6,4},{8,6},{10,8},{12,10},{14,12},{3,1},{5,3},{7,5},{... | collective-permute-start | bytes 294920 | tf_op jit(solution)/shard_map/while/body/eval_jaxpr/ppermute | solution.py:24
  89.9 5.6 %collective-permute-start.1 = (f32[6,2,1,2048]{3,2,1,0:T(1,128)S(1)}, f32[6,2,1,2048]{3,2,1,0:T(1,128)S(1)}, u32[]{:S(2)}, u32[]{:S(2)}) collective-permute-start(f32[6,2,1,2048]{3,2,1,0:T(1,128)S(1)} %get-tuple-element.354), channel_id=1, source_target_pairs={{0,2},{2,4},{4,6},{6,8},{8,10},{10,12},{12,14},{1,3},{3,5},{5,7},{... | collective-permute-start | bytes 294920 | tf_op jit(solution)/shard_map/while/body/eval_jaxpr/ppermute | solution.py:21
  118.1 6.3 %collective-permute-start = (f32[6,2,1,2048]{3,2,1,0:T(1,128)S(1)}, f32[6,2,1,2048]{3,2,1,0:T(1,128)S(1)}, u32[]{:S(2)}, u32[]{:S(2)}) collective-permute-start(f32[6,2,1,2048]{3,2,1,0:T(1,128)S(1)} %get-tuple-element.353), channel_id=1, source_target_pairs={{2,0},{4,2},{6,4},{8,6},{10,8},{12,10},{14,12},{3,1},{5,3},{7,5},{... | collective-permute-start | bytes 294920 | tf_op jit(solution)/shard_map/while/body/eval_jaxpr/ppermute | solution.py:24
  119.4 5.6 %collective-permute-start.1 = (f32[6,2,1,2048]{3,2,1,0:T(1,128)S(1)}, f32[6,2,1,2048]{3,2,1,0:T(1,128)S(1)}, u32[]{:S(2)}, u32[]{:S(2)}) collective-permute-start(f32[6,2,1,2048]{3,2,1,0:T(1,128)S(1)} %get-tuple-element.354), channel_id=1, source_target_pairs={{0,2},{2,4},{4,6},{6,8},{8,10},{10,12},{12,14},{1,3},{3,5},{5,7},{... | collective-permute-start | bytes 294920 | tf_op jit(solution)/shard_map/while/body/eval_jaxpr/ppermute | solution.py:21
  147.7 6.3 %collective-permute-start = (f32[6,2,1,2048]{3,2,1,0:T(1,128)S(1)}, f32[6,2,1,2048]{3,2,1,0:T(1,128)S(1)}, u32[]{:S(2)}, u32[]{:S(2)}) collective-permute-start(f32[6,2,1,2048]{3,2,1,0:T(1,128)S(1)} %get-tuple-element.353), channel_id=1, source_target_pairs={{2,0},{4,2},{6,4},{8,6},{10,8},{12,10},{14,12},{3,1},{5,3},{7,5},{... | collective-permute-start | bytes 294920 | tf_op jit(solution)/shard_map/while/body/eval_jaxpr/ppermute | solution.py:24
  149.0 5.6 %collective-permute-start.1 = (f32[6,2,1,2048]{3,2,1,0:T(1,128)S(1)}, f32[6,2,1,2048]{3,2,1,0:T(1,128)S(1)}, u32[]{:S(2)}, u32[]{:S(2)}) collective-permute-start(f32[6,2,1,2048]{3,2,1,0:T(1,128)S(1)} %get-tuple-element.354), channel_id=1, source_target_pairs={{0,2},{2,4},{4,6},{6,8},{8,10},{10,12},{12,14},{1,3},{3,5},{5,7},{... | collective-permute-start | bytes 294920 | tf_op jit(solution)/shard_map/while/body/eval_jaxpr/ppermute | solution.py:21
  177.2 6.3 %collective-permute-start = (f32[6,2,1,2048]{3,2,1,0:T(1,128)S(1)}, f32[6,2,1,2048]{3,2,1,0:T(1,128)S(1)}, u32[]{:S(2)}, u32[]{:S(2)}) collective-permute-start(f32[6,2,1,2048]{3,2,1,0:T(1,128)S(1)} %get-tuple-element.353), channel_id=1, source_target_pairs={{2,0},{4,2},{6,4},{8,6},{10,8},{12,10},{14,12},{3,1},{5,3},{7,5},{... | collective-permute-start | bytes 294920 | tf_op jit(solution)/shard_map/while/body/eval_jaxpr/ppermute | solution.py:24
  178.5 5.6 %collective-permute-start.1 = (f32[6,2,1,2048]{3,2,1,0:T(1,128)S(1)}, f32[6,2,1,2048]{3,2,1,0:T(1,128)S(1)}, u32[]{:S(2)}, u32[]{:S(2)}) collective-permute-start(f32[6,2,1,2048]{3,2,1,0:T(1,128)S(1)} %get-tuple-element.354), channel_id=1, source_target_pairs={{0,2},{2,4},{4,6},{6,8},{8,10},{10,12},{12,14},{1,3},{3,5},{5,7},{... | collective-permute-start | bytes 294920 | tf_op jit(solution)/shard_map/while/body/eval_jaxpr/ppermute | solution.py:21
  206.9 6.3 %collective-permute-start = (f32[6,2,1,2048]{3,2,1,0:T(1,128)S(1)}, f32[6,2,1,2048]{3,2,1,0:T(1,128)S(1)}, u32[]{:S(2)}, u32[]{:S(2)}) collective-permute-start(f32[6,2,1,2048]{3,2,1,0:T(1,128)S(1)} %get-tuple-element.353), channel_id=1, source_target_pairs={{2,0},{4,2},{6,4},{8,6},{10,8},{12,10},{14,12},{3,1},{5,3},{7,5},{... | collective-permute-start | bytes 294920 | tf_op jit(solution)/shard_map/while/body/eval_jaxpr/ppermute | solution.py:24
  208.2 5.6 %collective-permute-start.1 = (f32[6,2,1,2048]{3,2,1,0:T(1,128)S(1)}, f32[6,2,1,2048]{3,2,1,0:T(1,128)S(1)}, u32[]{:S(2)}, u32[]{:S(2)}) collective-permute-start(f32[6,2,1,2048]{3,2,1,0:T(1,128)S(1)} %get-tuple-element.354), channel_id=1, source_target_pairs={{0,2},{2,4},{4,6},{6,8},{8,10},{10,12},{12,14},{1,3},{3,5},{5,7},{... | collective-permute-start | bytes 294920 | tf_op jit(solution)/shard_map/while/body/eval_jaxpr/ppermute | solution.py:21
  236.4 6.3 %collective-permute-start = (f32[6,2,1,2048]{3,2,1,0:T(1,128)S(1)}, f32[6,2,1,2048]{3,2,1,0:T(1,128)S(1)}, u32[]{:S(2)}, u32[]{:S(2)}) collective-permute-start(f32[6,2,1,2048]{3,2,1,0:T(1,128)S(1)} %get-tuple-element.353), channel_id=1, source_target_pairs={{2,0},{4,2},{6,4},{8,6},{10,8},{12,10},{14,12},{3,1},{5,3},{7,5},{... | collective-permute-start | bytes 294920 | tf_op jit(solution)/shard_map/while/body/eval_jaxpr/ppermute | solution.py:24
  237.7 6.6 %collective-permute-start.1 = (f32[6,2,1,2048]{3,2,1,0:T(1,128)S(1)}, f32[6,2,1,2048]{3,2,1,0:T(1,128)S(1)}, u32[]{:S(2)}, u32[]{:S(2)}) collective-permute-start(f32[6,2,1,2048]{3,2,1,0:T(1,128)S(1)} %get-tuple-element.354), channel_id=1, source_target_pairs={{0,2},{2,4},{4,6},{6,8},{8,10},{10,12},{12,14},{1,3},{3,5},{5,7},{... | collective-permute-start | bytes 294920 | tf_op jit(solution)/shard_map/while/body/eval_jaxpr/ppermute | solution.py:21
  267.0 6.3 %collective-permute-start = (f32[6,2,1,2048]{3,2,1,0:T(1,128)S(1)}, f32[6,2,1,2048]{3,2,1,0:T(1,128)S(1)}, u32[]{:S(2)}, u32[]{:S(2)}) collective-permute-start(f32[6,2,1,2048]{3,2,1,0:T(1,128)S(1)} %get-tuple-element.353), channel_id=1, source_target_pairs={{2,0},{4,2},{6,4},{8,6},{10,8},{12,10},{14,12},{3,1},{5,3},{7,5},{... | collective-permute-start | bytes 294920 | tf_op jit(solution)/shard_map/while/body/eval_jaxpr/ppermute | solution.py:24
  268.3 5.6 %collective-permute-start.1 = (f32[6,2,1,2048]{3,2,1,0:T(1,128)S(1)}, f32[6,2,1,2048]{3,2,1,0:T(1,128)S(1)}, u32[]{:S(2)}, u32[]{:S(2)}) collective-permute-start(f32[6,2,1,2048]{3,2,1,0:T(1,128)S(1)} %get-tuple-element.354), channel_id=1, source_target_pairs={{0,2},{2,4},{4,6},{6,8},{8,10},{10,12},{12,14},{1,3},{3,5},{5,7},{... | collective-permute-start | bytes 294920 | tf_op jit(solution)/shard_map/while/body/eval_jaxpr/ppermute | solution.py:21
  296.5 6.3 %collective-permute-start = (f32[6,2,1,2048]{3,2,1,0:T(1,128)S(1)}, f32[6,2,1,2048]{3,2,1,0:T(1,128)S(1)}, u32[]{:S(2)}, u32[]{:S(2)}) collective-permute-start(f32[6,2,1,2048]{3,2,1,0:T(1,128)S(1)} %get-tuple-element.353), channel_id=1, source_target_pairs={{2,0},{4,2},{6,4},{8,6},{10,8},{12,10},{14,12},{3,1},{5,3},{7,5},{... | collective-permute-start | bytes 294920 | tf_op jit(solution)/shard_map/while/body/eval_jaxpr/ppermute | solution.py:24
  297.8 5.6 %collective-permute-start.1 = (f32[6,2,1,2048]{3,2,1,0:T(1,128)S(1)}, f32[6,2,1,2048]{3,2,1,0:T(1,128)S(1)}, u32[]{:S(2)}, u32[]{:S(2)}) collective-permute-start(f32[6,2,1,2048]{3,2,1,0:T(1,128)S(1)} %get-tuple-element.354), channel_id=1, source_target_pairs={{0,2},{2,4},{4,6},{6,8},{8,10},{10,12},{12,14},{1,3},{3,5},{5,7},{... | collective-permute-start | bytes 294920 | tf_op jit(solution)/shard_map/while/body/eval_jaxpr/ppermute | solution.py:21
  326.0 6.3 %collective-permute-start = (f32[6,2,1,2048]{3,2,1,0:T(1,128)S(1)}, f32[6,2,1,2048]{3,2,1,0:T(1,128)S(1)}, u32[]{:S(2)}, u32[]{:S(2)}) collective-permute-start(f32[6,2,1,2048]{3,2,1,0:T(1,128)S(1)} %get-tuple-element.353), channel_id=1, source_target_pairs={{2,0},{4,2},{6,4},{8,6},{10,8},{12,10},{14,12},{3,1},{5,3},{7,5},{... | collective-permute-start | bytes 294920 | tf_op jit(solution)/shard_map/while/body/eval_jaxpr/ppermute | solution.py:24
  327.3 5.6 %collective-permute-start.1 = (f32[6,2,1,2048]{3,2,1,0:T(1,128)S(1)}, f32[6,2,1,2048]{3,2,1,0:T(1,128)S(1)}, u32[]{:S(2)}, u32[]{:S(2)}) collective-permute-start(f32[6,2,1,2048]{3,2,1,0:T(1,128)S(1)} %get-tuple-element.354), channel_id=1, source_target_pairs={{0,2},{2,4},{4,6},{6,8},{8,10},{10,12},{12,14},{1,3},{3,5},{5,7},{... | collective-permute-start | bytes 294920 | tf_op jit(solution)/shard_map/while/body/eval_jaxpr/ppermute | solution.py:21
  355.8 6.3 %collective-permute-start = (f32[6,2,1,2048]{3,2,1,0:T(1,128)S(1)}, f32[6,2,1,2048]{3,2,1,0:T(1,128)S(1)}, u32[]{:S(2)}, u32[]{:S(2)}) collective-permute-start(f32[6,2,1,2048]{3,2,1,0:T(1,128)S(1)} %get-tuple-element.353), channel_id=1, source_target_pairs={{2,0},{4,2},{6,4},{8,6},{10,8},{12,10},{14,12},{3,1},{5,3},{7,5},{... | collective-permute-start | bytes 294920 | tf_op jit(solution)/shard_map/while/body/eval_jaxpr/ppermute | solution.py:24
  357.1 5.6 %collective-permute-start.1 = (f32[6,2,1,2048]{3,2,1,0:T(1,128)S(1)}, f32[6,2,1,2048]{3,2,1,0:T(1,128)S(1)}, u32[]{:S(2)}, u32[]{:S(2)}) collective-permute-start(f32[6,2,1,2048]{3,2,1,0:T(1,128)S(1)} %get-tuple-element.354), channel_id=1, source_target_pairs={{0,2},{2,4},{4,6},{6,8},{8,10},{10,12},{12,14},{1,3},{3,5},{5,7},{... | collective-permute-start | bytes 294920 | tf_op jit(solution)/shard_map/while/body/eval_jaxpr/ppermute | solution.py:21
  386.4 3.2 collective-permute-start.8
  388.0 5.4 %collective-permute-start.9 = (f32[6,2,1,2048]{3,2,1,0:T(1,128)S(1)}, f32[6,2,1,2048]{3,2,1,0:T(1,128)S(1)}, u32[]{:S(2)}, u32[]{:S(2)}) collective-permute-start(f32[6,2,1,2048]{3,2,1,0:T(1,128)S(1)} %get-tuple-element.245), channel_id=1, source_target_pairs={{2,0},{4,2},{6,4},{8,6},{10,8},{12,10},{14,12},{3,1},{5,3},{7,5},{... | collective-permute-start | bytes 294920 | tf_op jit(solution)/shard_map/ppermute | solution.py:24
  (48 other events, 181.1 us)
Sparse Core Ops, SparseCore 0:
  396.4 79.5 all-reduce.10
where the time goes:
time: 487 us; the launch traced here: 484 us
  blocking collectives  187 us (38%)
  waiting for transfers between devices  94.8 us (19%)
  other arithmetic  92.8 us (19%)
  starting transfers between devices  77.7 us (16%)
  local copies, waits for them, and re-layouts  16.7 us (3%)
  between operations  13.7 us (3%)
    psum x12, blocking collectives, both_sums(): lax.psum((inner_sums(vector, vector), inner_sums(vector, applied)), 'strip')  187 us
    psum x1, waiting for transfers between devices, per_device(): summed = lax.psum(local_sum, 'wave')  79.8 us
    ppermute x15, starting transfers between devices, padded_2(): lax.ppermute(lax.slice_in_dim(block, block.shape[dim] - width, None, axis...  58.3 us
    add x11, other arithmetic, iterate(): direction = residual + beta_ratio * direction  25 us
    reduce_sum x12, other arithmetic, inner_sums(): return jnp.sum(first * second, axis=(2, 3), keepdims=True)  23.1 us
    ppermute x15, starting transfers between devices, padded_2(): lax.ppermute(lax.slice_in_dim(block, 0, width, axis=dim), axis, backward)  19.4 us
    concatenate x15, other arithmetic, padded_2(): block = jnp.concatenate([low, block, high], axis=dim)  14.1 us
    mul x11, other arithmetic, operate(): result = diagonal * vector - face_up * padded[:, :, :-2, 1:-1]  10.7 us
  transfers between devices with their start and end apart: 31, of which 15 were waited for; matrix products, arithmetic and copies ran while one was open for 4% of the time, Pallas kernels for 0%

commit v1 on v0

--- a/solution.py
+++ b/solution.py
@@ -3,6 +3,8 @@
 import jax
 import jax.numpy as jnp
 from jax import lax
+from jax.experimental import pallas as pl
+from jax.experimental.pallas import tpu as pltpu
 from jax.sharding import PartitionSpec as P
 
 WAVES = 12
@@ -38,7 +40,7 @@
     return jnp.sum(first * second, axis=(2, 3), keepdims=True)
 
 
-def per_device(prior_fields, conductivity, electrode_nodes, source_pair, innovation):
+def per_device_strips(prior_fields, conductivity, electrode_nodes, source_pair, innovation):
     wave_dev = prior_fields.shape[0]
     row_count = prior_fields.shape[2]
     cell_count = prior_fields.shape[3]
@@ -131,6 +133,416 @@
     return -share_out
 
 
+LANES = 128
+PAD = 8
+ROWS = 64
+FIRST = 1
+
+
+def gathers_whole(shape):
+    waves, _, rows, cells = shape
+    strips = lax.axis_size("strip")
+    return (
+        lax.axis_size("wave") == 2
+        and 2 * rows * strips == LANES
+        and rows == PAD
+        and strips >= waves + FIRST
+        and cells % (2 * LANES) == 0
+    )
+
+
+def enter(peers):
+    barrier = pltpu.get_barrier_semaphore()
+    for peer in peers:
+        pl.semaphore_signal(barrier, inc=1, device_id=peer, device_id_type=pl.DeviceIdType.MESH)
+    pl.semaphore_wait(barrier, len(peers))
+
+
+def strip_peers():
+    strips = lax.axis_size("strip")
+    strip = lax.axis_index("strip")
+    return [{"strip": lax.rem(strip + hop, strips)} for hop in range(1, strips)]
+
+
+def gather_kernel(prior, sigma, fields, section, sent, got, sigma_sent, sigma_got, own):
+    strips = lax.axis_size("strip")
+    strip = lax.axis_index("strip")
+    waves = prior.shape[0]
+    rows = sigma.shape[0]
+    here = pl.ds(pl.multiple_of(strip * rows, PAD), rows)
+    enter(strip_peers())
+
+    def field_copy(place):
+        return pltpu.make_async_remote_copy(
+            src_ref=prior.at[place],
+            dst_ref=fields.at[:, here, :],
+            send_sem=sent.at[place],
+            recv_sem=got.at[strip],
+            device_id={"strip": place + FIRST},
+            device_id_type=pl.DeviceIdType.MESH,
+        )
+
+    def sigma_copy(place):
+        return pltpu.make_async_remote_copy(
+            src_ref=sigma,
+            dst_ref=section.at[here, :],
+            send_sem=sigma_sent.at[place],
+            recv_sem=sigma_got.at[strip],
+            device_id={"strip": place + FIRST},
+            device_id_type=pl.DeviceIdType.MESH,
+        )
+
+    def local_copies(place):
+        return (
+            pltpu.make_async_copy(prior.at[place], fields.at[:, here, :], own.at[0]),
+            pltpu.make_async_copy(sigma, section.at[here, :], own.at[1]),
+        )
+
+    for place in range(waves):
+
+        @pl.when(strip != place + FIRST)
+        def _():
+            sigma_copy(place).start()
+            field_copy(place).start()
+
+        @pl.when(strip == place + FIRST)
+        def _():
+            for copy in local_copies(place):
+                copy.start()
+
+    for place in range(waves):
+
+        @pl.when(strip != place + FIRST)
+        def _():
+            sigma_copy(place).wait_send()
+            field_copy(place).wait_send()
+
+        @pl.when(strip == place + FIRST)
+        def _():
+            for copy in local_copies(place):
+                copy.wait()
+            for source in range(strips):
+                if source != place + FIRST:
+                    there = pl.ds(source * rows, rows)
+                    pltpu.make_async_copy(
+                        section.at[there, :], section.at[there, :], sigma_got.at[source]
+                    ).wait()
+                    pltpu.make_async_copy(
+                        fields.at[:, there, :], fields.at[:, there, :], got.at[source]
+                    ).wait()
+
+
+def solve_kernel(
+    nodes, pair, gains, scales, fields, section, out, x, d, r, q, s, diag, up, down, left
+):
+    half = r.shape[1]
+    cells = 2 * half
+    count = nodes.shape[0]
+    step = 64
+    square = scales[0]
+    weight = scales[1]
+    lane = lax.broadcasted_iota(jnp.int32, (PAD, LANES), 1)
+    second = lane >= ROWS
+
+    def swap(block):
+        return pltpu.roll(block, ROWS, 1)
+
+    def edges(ref):
+        last = ref[pl.ds(half, PAD), :]
+        ref[pl.ds(0, PAD), :] = jnp.where(second, swap(last), 0.0)
+        first = ref[pl.ds(PAD, PAD), :]
+        ref[pl.ds(half + PAD, PAD), :] = jnp.where(second, 0.0, swap(first))
+
+    def turn(read, ref):
+        for block in range(half // LANES):
+            both = jnp.concatenate(
+                [read(pl.ds(block * LANES, LANES)), read(pl.ds(half + block * LANES, LANES))], 0
+            )
+            ref[pl.ds(PAD + block * LANES, LANES), :] = both.T
+
+    turn(lambda cols: section[:, cols], s)
+    edges(s)
+    for c in range(2):
+        turn(lambda cols, c=c: fields[c, :, cols], x.at[c])
+        edges(x.at[c])
+
+    row_lane = lax.rem(lax.broadcasted_iota(jnp.int32, (step, LANES), 1), ROWS)
+    top = row_lane == 0
+    bottom = row_lane == ROWS - 1
+
+    def rows(index, shift=0):
+        return pl.ds(index * step + shift, step)
+
+    @pl.loop(0, half // step)
+    def _(i):
+        here = s[rows(i, PAD), :]
+        face_left = 0.5 * (here + s[rows(i, PAD - 1), :])
+        face_right = 0.5 * (here + s[rows(i, PAD + 1), :])
+        face_up = jnp.where(top, 0.0, 0.5 * (here + pltpu.roll(here, 1, 1)))
+        below = jnp.where(bottom, 0.0, pltpu.roll(here, LANES - 1, 1))
+        face_down = 0.5 * (here + below)
+        diag[rows(i), :] = face_up + face_down + face_left + face_right + square * here
+        up[rows(i), :] = face_up
+        down[rows(i), :] = jnp.where(bottom, 0.0, face_down)
+        left[rows(i), :] = face_left
+        r[0, rows(i), :] = jnp.zeros_like(here)
+        r[1, rows(i), :] = jnp.zeros_like(here)
+
+    tail = s[pl.ds(half + PAD, PAD), :]
+    left[pl.ds(half, PAD), :] = 0.5 * (tail + s[pl.ds(half + PAD - 1, PAD), :])
+
+    line = lax.broadcasted_iota(jnp.int32, (1, LANES), 1)
+
+    def put(c, electrode, value):
+        node = nodes[electrode]
+        row = lax.div(node, cells)
+        col = lax.rem(node, cells)
+        side = lax.div(col, half)
+        at = pl.ds(lax.rem(col, half), 1)
+        r[c, at, :] = r[c, at, :] + jnp.where(line == side * ROWS + row, value, 0.0)
+
+    put(0, pair[0], 1.0)
+    put(0, pair[1], -1.0)
+
+    @pl.loop(0, count)
+    def _(electrode):
+        put(1, electrode, gains[electrode])
+
+    def applied(ref, c, i):
+        mid = ref[c, rows(i, PAD), :]
+        result = diag[rows(i), :] * mid - up[rows(i), :] * pltpu.roll(mid, 1, 1)
+        result = result - down[rows(i), :] * pltpu.roll(mid, LANES - 1, 1)
+        result = result - left[rows(i), :] * ref[c, rows(i, PAD - 1), :]
+        return mid, result - left[rows(i, 1), :] * ref[c, rows(i, PAD + 1), :]
+
+    def fold(value):
+        return jnp.sum(value.reshape(step // PAD, PAD, LANES), axis=0)
+
+    def total(value):
+        return jnp.sum(value, keepdims=True)
+
+    none = (jnp.zeros((PAD, LANES), jnp.float32),) * 2
+
+    def sweep(body, carry):
+        return lax.fori_loop(0, half // step, body, carry)
+
+    def start(i, sums):
+        found = []
+        for c in range(2):
+            _, image = applied(x, c, i)
+            value = r[c, rows(i), :] - image
+            r[c, rows(i), :] = value
+            d[c, rows(i, PAD), :] = value
+            found.append(sums[c] + fold(value * value))
+        return tuple(found)
+
+    norm = tuple(total(value) for value in sweep(start, none))
+
+    def images(i, sums):
+        found = []
+        for c in range(2):
+            mid, image = applied(d, c, i)
+            q[c, rows(i), :] = image
+            found.append(sums[c] + fold(mid * image))
+        return tuple(found)
+
+    def step_sizes(norm):
+        for c in range(2):
+            edges(d.at[c])
+        sums = sweep(images, none)
+        return tuple(norm[c] / total(sums[c]) for c in range(2))
+
+    def iterate(_, norm):
+        size = step_sizes(norm)
+
+        def reduce(i, sums):
+            found = []
+            for c in range(2):
+                value = r[c, rows(i), :] - size[c] * q[c, rows(i), :]
+                r[c, rows(i), :] = value
+                found.append(sums[c] + fold(value * value))
+            return tuple(found)
+
+        after = tuple(total(value) for value in sweep(reduce, none))
+        ratio = tuple(after[c] / norm[c] for c in range(2))
+
+        @pl.loop(0, half // step)
+        def _(i):
+            for c in range(2):
+                old = d[c, rows(i, PAD), :]
+                x[c, rows(i, PAD), :] = x[c, rows(i, PAD), :] + size[c] * old
+                d[c, rows(i, PAD), :] = r[c, rows(i), :] + ratio[c] * old
+
+        return after
+
+    norm = lax.fori_loop(0, ITERS - 1, iterate, norm)
+    size = step_sizes(norm)
+
+    @pl.loop(0, half // step)
+    def _(i):
+        for c in range(2):
+            x[c, rows(i, PAD), :] = x[c, rows(i, PAD), :] + size[c] * d[c, rows(i, PAD), :]
+
+    for c in range(2):
+        edges(x.at[c])
+
+    wide = lax.rem(lax.broadcasted_iota(jnp.int32, (LANES, LANES), 1), ROWS)
+
+    @pl.loop(0, half // LANES)
+    def _(b):
+        base = pl.multiple_of(b * LANES, LANES)
+        u = x[0, pl.ds(base + PAD, LANES), :]
+        v = x[1, pl.ds(base + PAD, LANES), :]
+        both = u * v
+        term = (u - x[0, pl.ds(base + PAD - 1, LANES), :]) * (
+            v - x[1, pl.ds(base + PAD - 1, LANES), :]
+        )
+        term = term + (u - x[0, pl.ds(base + PAD + 1, LANES), :]) * (
+            v - x[1, pl.ds(base + PAD + 1, LANES), :]
+        )
+        rise = (u - pltpu.roll(u, 1, 1)) * (v - pltpu.roll(v, 1, 1))
+        term = term + jnp.where(wide == 0, 0.0, rise)
+        term = term + jnp.where(wide == ROWS - 1, both, pltpu.roll(rise, LANES - 1, 1))
+        out[:, pl.ds(base, LANES)] = ((-weight) * (square * both + 0.5 * term)).T
+
+
+def scatter_kernel(own, out, other, mine, parts, core_sent, core_got, sent, got):
+    strips = lax.axis_size("strip")
+    strip = lax.axis_index("strip")
+    core = lax.axis_index("wave")
+    waves = parts.shape[0]
+    rows = out.shape[0]
+    enter(strip_peers() + [{"wave": 1 - core}])
+    solver = (strip >= FIRST) & (strip < FIRST + waves)
+
+    swap = pltpu.make_async_remote_copy(
+        src_ref=own.at[pl.ds(pl.multiple_of((1 - core) * ROWS, ROWS), ROWS), :],
+        dst_ref=other,
+        send_sem=core_sent,
+        recv_sem=core_got,
+        device_id={"wave": 1 - core},
+        device_id_type=pl.DeviceIdType.MESH,
+    )
+
+    def part_copy(target):
+        return pltpu.make_async_remote_copy(
+            src_ref=mine.at[pl.ds(target * rows, rows), :],
+            dst_ref=parts.at[strip - FIRST],
+            send_sem=sent.at[target],
+            recv_sem=got.at[strip - FIRST],
+            device_id={"strip": target},
+            device_id_type=pl.DeviceIdType.MESH,
+        )
+
+    @pl.when(solver)
+    def _():
+        swap.start()
+        swap.wait_recv()
+        mine[...] = own[pl.ds(pl.multiple_of(core * ROWS, ROWS), ROWS), :] + other[...]
+        for target in range(strips):
+
+            @pl.when(strip != target)
+            def _():
+                part_copy(target).start()
+
+        parts[strip - FIRST] = mine[pl.ds(pl.multiple_of(strip * rows, rows), rows), :]
+
+    for place in range(waves):
+
+        @pl.when(strip != place + FIRST)
+        def _():
+            pltpu.make_async_copy(parts.at[place], parts.at[place], got.at[place]).wait()
+
+    total = parts[0]
+    for place in range(1, waves):
+        total = total + parts[place]
+    out[...] = total
+
+    @pl.when(solver)
+    def _():
+        swap.wait_send()
+        for target in range(strips):
+
+            @pl.when(strip != target)
+            def _():
+                part_copy(target).wait_send()
+
+
+def per_device_whole(prior_fields, conductivity, electrode_nodes, source_pair, innovation):
+    waves, _, rows, cells = prior_fields.shape
+    strips = lax.axis_size("strip")
+    half = cells // 2
+    vmem = pl.BlockSpec(memory_space=pltpu.VMEM)
+    smem = pl.BlockSpec(memory_space=pltpu.SMEM)
+    f32 = jnp.float32
+    dma = pltpu.SemaphoreType.DMA
+
+    fields, section = pl.pallas_call(
+        gather_kernel,
+        out_shape=(
+            jax.ShapeDtypeStruct((2, ROWS, cells), f32),
+            jax.ShapeDtypeStruct((ROWS, cells), f32),
+        ),
+        in_specs=[vmem, vmem],
+        out_specs=(vmem, vmem),
+        scratch_shapes=[
+            dma((waves,)),
+            dma((strips,)),
+            dma((waves,)),
+            dma((strips,)),
+            dma((2,)),
+        ],
+        compiler_params=pltpu.CompilerParams(
+            collective_id=0, has_side_effects=True, vmem_limit_bytes=32 * 2**20
+        ),
+        name="gather_sections",
+    )(prior_fields, conductivity)
+
+    wave_id = lax.axis_index("wave") * waves + lax.axis_index("strip") - FIRST
+    wavenum, weights = wave_table(wave_id.astype(f32))
+    scales = jnp.stack([wavenum * wavenum, weights])
+    padded = half + 2 * PAD
+    partial = pl.pallas_call(
+        solve_kernel,
+        out_shape=jax.ShapeDtypeStruct((LANES, half), f32),
+        in_specs=[smem] * 4 + [vmem] * 2,
+        out_specs=vmem,
+        scratch_shapes=[
+            pltpu.VMEM((2, padded, LANES), f32),
+            pltpu.VMEM((2, padded, LANES), f32),
+            pltpu.VMEM((2, half, LANES), f32),
+            pltpu.VMEM((2, half, LANES), f32),
+            pltpu.VMEM((padded, LANES), f32),
+            pltpu.VMEM((half, LANES), f32),
+            pltpu.VMEM((half, LANES), f32),
+            pltpu.VMEM((half, LANES), f32),
+            pltpu.VMEM((half + PAD, LANES), f32),
+        ],
+        compiler_params=pltpu.CompilerParams(vmem_limit_bytes=32 * 2**20),
+        name="solve_wave",
+    )(electrode_nodes, source_pair, innovation, scales, fields, section)
+
+    return pl.pallas_call(
+        scatter_kernel,
+        out_shape=jax.ShapeDtypeStruct((rows, half), f32),
+        in_specs=[vmem],
+        out_specs=vmem,
+        scratch_shapes=[
+            pltpu.VMEM((ROWS, half), f32),
+            pltpu.VMEM((ROWS, half), f32),
+            pltpu.VMEM((waves, rows, half), f32),
+            dma,
+            dma,
+            dma((strips,)),
+            dma((waves,)),
+        ],
+        compiler_params=pltpu.CompilerParams(
+            collective_id=1, has_side_effects=True, vmem_limit_bytes=32 * 2**20
+        ),
+        name="scatter_gradient",
+    )(partial)
+
+
 def solution(mesh):
     in_specs = (
         P("wave", None, ("lines", "strip"), None),
@@ -140,6 +552,12 @@
         P("lines"),
     )
     out_specs = P(("lines", "strip"), "wave")
+
+    def per_device(prior_fields, *rest):
+        if gathers_whole(prior_fields.shape):
+            return per_device_whole(prior_fields, *rest)
+        return per_device_strips(prior_fields, *rest)
+
     return jax.shard_map(
         per_device, mesh=mesh, in_specs=in_specs, out_specs=out_specs, check_vma=False
     )

time: 487 us -> 83.6 us (0.17)
  blocking collectives: 187 us -> 0 us
  waiting for transfers between devices: 94.8 us -> 0 us
  other arithmetic: 92.8 us -> 0.08 us
  Pallas kernels: 0 us -> 80 us
  starting transfers between devices: 77.7 us -> 0 us
  between operations: 13.7 us -> 0.1 us
  local copies, waits for them, and re-layouts: 16.7 us -> 3.25 us
    psum x12 -> x0, blocking collectives: 187 us -> none  [both_sums(): lax.psum((inner_sums(vector, vector), inner_sums(vector, applied)), 'strip')]
    pallas_call x0 -> x3, Pallas kernels: none -> 80 us  [the longest x1 38.7 us: per_device_whole(): pl.pallas_call(solve_kernel, out_shape=jax.ShapeDtypeStruct((LANES, half)...]
    psum x1 -> x0, waiting for transfers between devices: 79.8 us -> none  [per_device(): summed = lax.psum(local_sum, 'wave')]
    ppermute x30 -> x0, starting transfers between devices: 77.7 us -> none  [the longest x15 58.3 us: padded_2(): lax.ppermute(lax.slice_in_dim(block, block.shape[dim] - width, None, axis...]
    add x15 -> x0, other arithmetic: 28.9 us -> none  [the longest x11 25 us: iterate(): direction = residual + beta_ratio * direction]
    reduce_sum x13 -> x0, other arithmetic: 24.5 us -> none  [the longest x12 23.1 us: inner_sums(): return jnp.sum(first * second, axis=(2, 3), keepdims=True)]
    ppermute x30 -> x0, waiting for transfers between devices: 15 us -> none  [the longest x15 8.08 us: padded_2(): lax.ppermute(lax.slice_in_dim(block, block.shape[dim] - width, None, axis...]
    concatenate x15 -> x0, other arithmetic: 14.1 us -> none  [padded_2(): block = jnp.concatenate([low, block, high], axis=dim)]
  transfers between devices with their start and end apart: 31 -> 0, of which waited for: 15 -> 0; matrix products, arithmetic and copies ran while one was open for 4% -> 0% of each run, Pallas kernels for 0% -> 0%
where the time goes in v1:
time: 83.6 us; the launch traced here: 83.4 us
  Pallas kernels  80 us (96%)
  local copies, waits for them, and re-layouts  3.25 us (4%)
    pallas_call x1, Pallas kernels, per_device_whole(): pl.pallas_call(solve_kernel, out_shape=jax.ShapeDtypeStruct((LANES, half)...  38.7 us
    pallas_call x1, Pallas kernels, per_device_whole(): pl.pallas_call(gather_kernel, out_shape=(jax.ShapeDtypeStruct((2, ROWS, c...  26 us
    pallas_call x1, Pallas kernels, per_device_whole(): pl.pallas_call(scatter_kernel, out_shape=jax.ShapeDtypeStruct((rows, half...  15.3 us
    unnamed x11, local copies, waits for them, and re-layouts  3.25 us

profile of v1, /device:TPU:1, one launch (start us, length us, event | category | flops | bytes accessed | tf_op | source)
XLA Modules:
  0.0 83.4 jit_solution(5484716445949358785)
XLA Ops:
  0.1 0.1 pad_maximum_fusion.scales
  0.1 0.0 copy-start
  0.1 1.1 %copy-done = f32[6,2,8,2048]{3,2,1,0:T(8,128)S(1)} copy-done((f32[6,2,8,2048]{3,2,1,0:T(8,128)S(1)}, f32[6,2,8,2048]{3,2,1,0:T(8,128)}, u32[]{:S(2)}) %copy-start) | copy-done | bytes 786456
  1.3 0.0 copy-start.1
  1.3 0.8 %copy-done.1 = f32[8,2048]{1,0:T(8,128)S(1)} copy-done((f32[8,2048]{1,0:T(8,128)S(1)}, f32[8,2048]{1,0:T(8,128)}, u32[]{:S(2)}) %copy-start.1) | copy-done | bytes 65560
  2.1 26.0 %gather_sections.1 = (f32[2,64,2048]{2,1,0:T(8,128)S(1)}, f32[64,2048]{1,0:T(8,128)S(1)}) custom-call(f32[6,2,8,2048]{3,2,1,0:T(8,128)S(1)} %copy-done, f32[8,2048]{1,0:T(8,128)S(1)} %copy-done.1), custom_call_target="tpu_custom_call" | custom-call | tf_op jit(solution)/shard_map/gather_sections/pallas_call | solution.py:480
  28.1 0.0 copy-start.2
  28.1 0.0 copy-start.3
  28.1 0.0 copy-start.4
  28.1 0.6 copy-done.2
  28.7 0.0 copy-done.3
  28.8 0.0 copy-done.4
  28.8 38.7 %solve_wave.1.own = f32[128,1024]{1,0:T(8,128)S(1)} custom-call(s32[64]{0:T(128)S(1)} %copy-done.2, s32[2]{0:T(128)S(1)} %copy-done.3, f32[64]{0:T(128)S(1)} %copy-done.4, f32[2]{0:T(128)S(1)} %pad_maximum_fusion.scales, f32[2,64,2048]{2,1,0:T(8,128)S(1)} %get-tuple-element.7.fields, f32[64,2048]{1,0:T(8,128)S(1)} %get-tuple-element.8.section), custom_call_target="tpu_custom_call" | custom-call | tf_op jit(solution)/shard_map/solve_wave/pallas_call | solution.py:505
  67.5 15.3 %scatter_gradient.1 = f32[8,1024]{1,0:T(8,128)S(1)} custom-call(f32[128,1024]{1,0:T(8,128)S(1)} %solve_wave.1.own), custom_call_target="tpu_custom_call" | custom-call | tf_op jit(solution)/shard_map/scatter_gradient/pallas_call | solution.py:525
  82.8 0.6 copy.7
Async XLA Ops:
  0.1 1.1 %copy-start = (f32[6,2,8,2048]{3,2,1,0:T(8,128)S(1)}, f32[6,2,8,2048]{3,2,1,0:T(8,128)}, u32[]{:S(2)}) copy-start(f32[6,2,8,2048]{3,2,1,0:T(8,128)} %prior.1) | copy-start | bytes 2359300
  1.3 0.8 %copy-start.1 = (f32[8,2048]{1,0:T(8,128)S(1)}, f32[8,2048]{1,0:T(8,128)}, u32[]{:S(2)}) copy-start(f32[8,2048]{1,0:T(8,128)} %sigma.1) | copy-start | bytes 196612
  28.1 0.7 copy-start.2
  28.1 0.7 copy-start.3
  28.1 0.7 copy-start.4

commit v2 on v0

--- a/solution.py
+++ b/solution.py
@@ -3,6 +3,8 @@
 import jax
 import jax.numpy as jnp
 from jax import lax
+from jax.experimental import pallas as pl
+from jax.experimental.pallas import tpu as pltpu
 from jax.sharding import PartitionSpec as P
 
 WAVES = 12
@@ -38,7 +40,7 @@
     return jnp.sum(first * second, axis=(2, 3), keepdims=True)
 
 
-def per_device(prior_fields, conductivity, electrode_nodes, source_pair, innovation):
+def per_device_strips(prior_fields, conductivity, electrode_nodes, source_pair, innovation):
     wave_dev = prior_fields.shape[0]
     row_count = prior_fields.shape[2]
     cell_count = prior_fields.shape[3]
@@ -131,6 +133,414 @@
     return -share_out
 
 
+LANES = 128
+PAD = 8
+ROWS = 64
+FIRST = 1
+STEP = 128
+
+
+def gathers_whole(shape, electrodes):
+    waves, _, rows, cells = shape
+    strips = lax.axis_size("strip")
+    return (
+        lax.axis_size("wave") == 2
+        and rows * strips == ROWS
+        and rows == PAD
+        and strips >= waves + FIRST
+        and cells % (2 * STEP) == 0
+        and cells // 2 >= 4 * STEP
+        and electrodes <= LANES
+    )
+
+
+def whole_kernel(
+    nodes, pair, gains, scales, prior, sigma, out,
+    fields, section, x, past, q, w, s, diag, up, left, charge, steps, grad, other, mine, parts,
+    sigma_sent, sigma_got, field_sent, field_got, own_sem, core_sent, core_got, sent, got,
+):
+    strips = lax.axis_size("strip")
+    strip = lax.axis_index("strip")
+    core = lax.axis_index("wave")
+    waves = prior.shape[0]
+    depth = sigma.shape[0]
+    half = q.shape[0]
+    cells = 2 * half
+    blocks = half // STEP
+    here = pl.ds(pl.multiple_of(strip * depth, PAD), depth)
+    peer = {"wave": 1 - core}
+    mesh_id = pl.DeviceIdType.MESH
+    solver = (strip >= FIRST) & (strip < FIRST + waves)
+
+    barrier = pltpu.get_barrier_semaphore()
+    for hop in range(1, strips):
+        pl.semaphore_signal(
+            barrier, inc=1, device_id={"strip": lax.rem(strip + hop, strips)}, device_id_type=mesh_id
+        )
+    pl.semaphore_signal(barrier, inc=1, device_id=peer, device_id_type=mesh_id)
+    pl.semaphore_wait(barrier, strips)
+
+    def remote(src, dst, send_sem, recv_sem, device):
+        return pltpu.make_async_remote_copy(
+            src_ref=src,
+            dst_ref=dst,
+            send_sem=send_sem,
+            recv_sem=recv_sem,
+            device_id=device,
+            device_id_type=mesh_id,
+        )
+
+    my_side = pl.ds(pl.multiple_of(core * half, LANES), half)
+
+    def sigma_copy(place):
+        return remote(
+            sigma.at[:, my_side],
+            section.at[core, here, :],
+            sigma_sent.at[place],
+            sigma_got.at[strip],
+            {"strip": place + FIRST},
+        )
+
+    def field_copy(place, c):
+        return remote(
+            prior.at[place, c],
+            fields.at[c, here, :],
+            field_sent.at[c, place],
+            field_got.at[c, strip],
+            {"strip": place + FIRST},
+        )
+
+    def own_sigma():
+        return pltpu.make_async_copy(
+            sigma.at[:, my_side], section.at[core, here, :], own_sem.at[2]
+        )
+
+    def own_field(c):
+        return pltpu.make_async_copy(
+            prior.at[strip - FIRST, c], fields.at[c, here, :], own_sem.at[c]
+        )
+
+    def each_other(body):
+        for place in range(waves):
+
+            @pl.when(strip != place + FIRST)
+            def _(place=place):
+                body(place)
+
+    def from_others(body):
+        for source in range(strips):
+
+            @pl.when(strip != source)
+            def _(source=source):
+                body(source)
+
+    def await_block(ref, sem):
+        pltpu.make_async_copy(ref, ref, sem).wait()
+
+    each_other(lambda place: sigma_copy(place).start())
+    each_other(lambda place: field_copy(place, 0).start())
+
+    @pl.when(solver)
+    def _():
+        own_sigma().start()
+        own_field(0).start()
+        own_field(1).start()
+
+    def send_second():
+        each_other(lambda place: sigma_copy(place).wait_send())
+        each_other(lambda place: field_copy(place, 0).wait_send())
+        each_other(lambda place: field_copy(place, 1).start())
+
+    square = scales[0]
+    weight = scales[1]
+    lane = lax.broadcasted_iota(jnp.int32, (PAD, LANES), 1)
+    second = lane >= ROWS
+
+    def swap(block):
+        return pltpu.roll(block, ROWS, 1)
+
+    def edges(ref):
+        last = ref[pl.ds(half, PAD), :]
+        ref[pl.ds(0, PAD), :] = jnp.where(second, swap(last), 0.0)
+        first = ref[pl.ds(PAD, PAD), :]
+        ref[pl.ds(half + PAD, PAD), :] = jnp.where(second, 0.0, swap(first))
+
+    def rows(block, shift=0):
+        return pl.ds(block * STEP + shift, STEP)
+
+    def fold(value):
+        return jnp.sum(value.reshape(STEP // PAD, PAD, LANES), axis=0)
+
+    def total(value):
+        return jnp.sum(value, keepdims=True)
+
+    def charges():
+        line = lax.broadcasted_iota(jnp.int32, (1, LANES), 1)
+        charge[...] = jnp.zeros_like(charge)
+
+        def mark(e, spots):
+            node = nodes[e]
+            col = lax.rem(node, cells)
+            side = lax.div(col, half)
+            hit = line == side * ROWS + lax.div(node, cells)
+            sign = jnp.where(pair[0] == e, 1.0, 0.0) - jnp.where(pair[1] == e, 1.0, 0.0)
+            charge[0, pl.ds(e, 1), :] = jnp.where(hit, sign, 0.0)
+            charge[1, pl.ds(e, 1), :] = jnp.where(hit, gains[e], 0.0)
+            return jnp.where(line == e, lax.rem(col, half), spots)
+
+        return lax.fori_loop(0, nodes.shape[0], mark, jnp.full((1, LANES), -1, jnp.int32))
+
+    def coefficients():
+        row_lane = lax.rem(lax.broadcasted_iota(jnp.int32, (STEP, LANES), 1), ROWS)
+        top = row_lane == 0
+        bottom = row_lane == ROWS - 1
+        for b in range(blocks):
+            cols = pl.ds(b * STEP, STEP)
+            s[rows(b, PAD), :] = jnp.concatenate([section[0, :, cols], section[1, :, cols]], 0).T
+        edges(s)
+        for b in range(blocks):
+            mid = s[rows(b, PAD), :]
+            face_left = 0.5 * (mid + s[rows(b, PAD - 1), :])
+            face_right = 0.5 * (mid + s[rows(b, PAD + 1), :])
+            up[rows(b), :] = jnp.where(top, 0.0, 0.5 * (mid + pltpu.roll(mid, 1, 1)))
+            left[rows(b), :] = face_left
+            floor = jnp.where(bottom, 0.5 * mid, 0.0)
+            diag[rows(b), :] = face_left + face_right + floor + square * mid
+        tail = s[pl.ds(half + PAD, PAD), :]
+        left[pl.ds(half, PAD), :] = 0.5 * (tail + s[pl.ds(half + PAD - 1, PAD), :])
+
+    def applied(ref, b):
+        mid = ref[rows(b, PAD), :]
+        flux = up[rows(b), :] * (mid - pltpu.roll(mid, 1, 1))
+        result = diag[rows(b), :] * mid + (flux - pltpu.roll(flux, LANES - 1, 1))
+        result = result - left[rows(b), :] * ref[rows(b, PAD - 1), :]
+        return mid, result - left[rows(b, 1), :] * ref[rows(b, PAD + 1), :]
+
+    def solve(c, spots):
+        xc = x.at[c]
+        for b in range(blocks):
+            one = fields[c, :, pl.ds(b * STEP, STEP)]
+            two = fields[c, :, pl.ds(half + b * STEP, STEP)]
+            xc[rows(b, PAD), :] = jnp.concatenate([one, two], 0).T
+        edges(xc)
+        for b in range(blocks):
+            cell = b * STEP + lax.broadcasted_iota(jnp.int32, (STEP, LANES), 0)
+            source = jnp.dot(
+                jnp.where(cell == spots, 1.0, 0.0),
+                charge[c],
+                precision=lax.Precision.HIGHEST,
+                preferred_element_type=jnp.float32,
+            )
+            past[0, rows(b, PAD), :] = source - applied(xc, b)[1]
+        edges(past.at[0])
+
+        def image(ref, b, sums):
+            mid, value = applied(ref, b)
+            w[rows(b), :] = value
+            return sums[0] + fold(mid * mid), sums[1] + fold(mid * value)
+
+        none = (jnp.zeros((PAD, LANES), jnp.float32),) * 2
+        sums = none
+        for b in range(blocks):
+            sums = image(past.at[0], b, sums)
+        norm, product = total(sums[0]), total(sums[1])
+        size = norm / product
+        for b in range(blocks):
+            q[rows(b), :] = jnp.zeros((STEP, LANES), jnp.float32)
+
+        def wide(value):
+            return jnp.broadcast_to(value, (1, LANES))
+
+        steps[0, pl.ds(0, 1), :] = wide(size)
+
+        def iterate(k, carry):
+            norm, size, ratio = carry
+            now = past.at[k]
+            new = past.at[k + 1]
+
+            def advance(b):
+                along = w[rows(b), :] + ratio * q[rows(b), :]
+                q[rows(b), :] = along
+                new[rows(b, PAD), :] = now[rows(b, PAD), :] - size * along
+
+            advance(blocks - 1)
+            advance(0)
+            edges(new)
+            sums = none
+            for b in range(blocks):
+                if b + 1 < blocks - 1:
+                    advance(b + 1)
+                sums = image(new, b, sums)
+            after, product = total(sums[0]), total(sums[1])
+            ratio = after / norm
+            size = after / (product - ratio * after / size)
+            steps[0, pl.ds(k + 1, 1), :] = wide(size)
+            steps[1, pl.ds(k + 1, 1), :] = wide(ratio)
+            return after, size, ratio
+
+        lax.fori_loop(0, ITERS - 1, iterate, (norm, size, jnp.zeros_like(norm)))
+        gain = steps[0, pl.ds(ITERS - 1, 1), :]
+        shares = [gain]
+        for k in range(ITERS - 2, -1, -1):
+            gain = steps[0, pl.ds(k, 1), :] + steps[1, pl.ds(k + 1, 1), :] * gain
+            shares.insert(0, gain)
+        for b in range(blocks):
+            value = xc[rows(b, PAD), :]
+            for k in range(ITERS):
+                value = value + shares[k] * past[k, rows(b, PAD), :]
+            xc[rows(b, PAD), :] = value
+        edges(xc)
+
+    core_swap = remote(section.at[core], section.at[core], core_sent.at[0], core_got.at[0], peer)
+    grad_swap = remote(
+        grad.at[pl.ds(pl.multiple_of((1 - core) * ROWS, ROWS), ROWS), :],
+        other,
+        core_sent.at[1],
+        core_got.at[1],
+        peer,
+    )
+
+    def part_copy(target):
+        return remote(
+            mine.at[pl.ds(target * depth, depth), :],
+            parts.at[strip - FIRST],
+            sent.at[target],
+            got.at[strip - FIRST],
+            {"strip": target},
+        )
+
+    @pl.when(jnp.logical_not(solver))
+    def _():
+        send_second()
+
+    @pl.when(solver)
+    def _():
+        spots = charges()
+        own_sigma().wait()
+        from_others(
+            lambda source: await_block(
+                section.at[core, pl.ds(source * depth, depth), :], sigma_got.at[source]
+            )
+        )
+        core_swap.start()
+        core_swap.wait()
+        coefficients()
+        own_field(0).wait()
+        from_others(
+            lambda source: await_block(
+                fields.at[0, pl.ds(source * depth, depth), :], field_got.at[0, source]
+            )
+        )
+        send_second()
+        solve(0, spots)
+        own_field(1).wait()
+        from_others(
+            lambda source: await_block(
+                fields.at[1, pl.ds(source * depth, depth), :], field_got.at[1, source]
+            )
+        )
+        solve(1, spots)
+
+        row_lane = lax.rem(lax.broadcasted_iota(jnp.int32, (STEP, LANES), 1), ROWS)
+        for b in range(blocks):
+            u = x[0, rows(b, PAD), :]
+            v = x[1, rows(b, PAD), :]
+            both = u * v
+            term = (u - x[0, rows(b, PAD - 1), :]) * (v - x[1, rows(b, PAD - 1), :])
+            term = term + (u - x[0, rows(b, PAD + 1), :]) * (v - x[1, rows(b, PAD + 1), :])
+            rise = (u - pltpu.roll(u, 1, 1)) * (v - pltpu.roll(v, 1, 1))
+            term = term + jnp.where(row_lane == 0, 0.0, rise)
+            fall = pltpu.roll(rise, LANES - 1, 1)
+            term = term + jnp.where(row_lane == ROWS - 1, both, fall)
+            grad[:, pl.ds(b * STEP, STEP)] = ((-weight) * (square * both + 0.5 * term)).T
+
+        grad_swap.start()
+        grad_swap.wait_recv()
+        mine[...] = grad[pl.ds(pl.multiple_of(core * ROWS, ROWS), ROWS), :] + other[...]
+        for target in range(strips):
+
+            @pl.when(strip != target)
+            def _():
+                part_copy(target).start()
+
+        parts[strip - FIRST] = mine[here, :]
+
+    for place in range(waves):
+
+        @pl.when(strip != place + FIRST)
+        def _():
+            await_block(parts.at[place], got.at[place])
+
+    result = parts[0]
+    for place in range(1, waves):
+        result = result + parts[place]
+    out[...] = result
+
+    each_other(lambda place: field_copy(place, 1).wait_send())
+
+    @pl.when(solver)
+    def _():
+        grad_swap.wait_send()
+        for target in range(strips):
+
+            @pl.when(strip != target)
+            def _():
+                part_copy(target).wait_send()
+
+
+def per_device_whole(prior_fields, conductivity, electrode_nodes, source_pair, innovation):
+    waves, _, rows, cells = prior_fields.shape
+    strips = lax.axis_size("strip")
+    half = cells // 2
+    padded = half + 2 * PAD
+    vmem = pl.BlockSpec(memory_space=pltpu.VMEM)
+    smem = pl.BlockSpec(memory_space=pltpu.SMEM)
+    anywhere = pl.BlockSpec(memory_space=pl.ANY)
+    f32 = jnp.float32
+    dma = pltpu.SemaphoreType.DMA
+
+    wave_id = lax.axis_index("wave") * waves + lax.axis_index("strip") - FIRST
+    wavenum, weights = wave_table(wave_id.astype(f32))
+    scales = jnp.stack([wavenum * wavenum, weights])
+    return pl.pallas_call(
+        whole_kernel,
+        out_shape=jax.ShapeDtypeStruct((rows, half), f32),
+        in_specs=[smem] * 4 + [anywhere] * 2,
+        out_specs=vmem,
+        scratch_shapes=[
+            pltpu.VMEM((2, ROWS, cells), f32),
+            pltpu.VMEM((2, ROWS, half), f32),
+            pltpu.VMEM((2, padded, LANES), f32),
+            pltpu.VMEM((ITERS, padded, LANES), f32),
+            pltpu.VMEM((half, LANES), f32),
+            pltpu.VMEM((half, LANES), f32),
+            pltpu.VMEM((padded, LANES), f32),
+            pltpu.VMEM((half, LANES), f32),
+            pltpu.VMEM((half, LANES), f32),
+            pltpu.VMEM((half + PAD, LANES), f32),
+            pltpu.VMEM((2, LANES, LANES), f32),
+            pltpu.VMEM((2, 2 * PAD, LANES), f32),
+            pltpu.VMEM((LANES, half), f32),
+            pltpu.VMEM((ROWS, half), f32),
+            pltpu.VMEM((ROWS, half), f32),
+            pltpu.VMEM((waves, rows, half), f32),
+            dma((waves,)),
+            dma((strips,)),
+            dma((2, waves)),
+            dma((2, strips)),
+            dma((3,)),
+            dma((2,)),
+            dma((2,)),
+            dma((strips,)),
+            dma((waves,)),
+        ],
+        compiler_params=pltpu.CompilerParams(
+            collective_id=0, has_side_effects=True, vmem_limit_bytes=40 * 2**20
+        ),
+        name="solve_wave",
+    )(electrode_nodes, source_pair, innovation, scales, prior_fields, conductivity)
+
+
 def solution(mesh):
     in_specs = (
         P("wave", None, ("lines", "strip"), None),
@@ -140,6 +550,12 @@
         P("lines"),
     )
     out_specs = P(("lines", "strip"), "wave")
+
+    def per_device(prior_fields, *rest):
+        if gathers_whole(prior_fields.shape, rest[-1].shape[0]):
+            return per_device_whole(prior_fields, *rest)
+        return per_device_strips(prior_fields, *rest)
+
     return jax.shard_map(
         per_device, mesh=mesh, in_specs=in_specs, out_specs=out_specs, check_vma=False
     )

time: 487 us -> 52.8 us (0.11)
  blocking collectives: 187 us -> 0 us
  waiting for transfers between devices: 94.8 us -> 0 us
  other arithmetic: 92.8 us -> 0.08 us
  starting transfers between devices: 77.7 us -> 0 us
  Pallas kernels: 0 us -> 49.3 us
  between operations: 13.7 us -> 0.09 us
  local copies, waits for them, and re-layouts: 16.7 us -> 3.18 us
    psum x12 -> x0, blocking collectives: 187 us -> none  [both_sums(): lax.psum((inner_sums(vector, vector), inner_sums(vector, applied)), 'strip')]
    psum x1 -> x0, waiting for transfers between devices: 79.8 us -> none  [per_device(): summed = lax.psum(local_sum, 'wave')]
    ppermute x30 -> x0, starting transfers between devices: 77.7 us -> none  [the longest x15 58.3 us: padded_2(): lax.ppermute(lax.slice_in_dim(block, block.shape[dim] - width, None, axis...]
    pallas_call x0 -> x1, Pallas kernels: none -> 49.3 us  [per_device_whole(): pl.pallas_call(whole_kernel, out_shape=jax.ShapeDtypeStruct((rows, half),...]
    add x15 -> x0, other arithmetic: 28.9 us -> none  [the longest x11 25 us: iterate(): direction = residual + beta_ratio * direction]
    reduce_sum x13 -> x0, other arithmetic: 24.5 us -> none  [the longest x12 23.1 us: inner_sums(): return jnp.sum(first * second, axis=(2, 3), keepdims=True)]
    ppermute x30 -> x0, waiting for transfers between devices: 15 us -> none  [the longest x15 8.08 us: padded_2(): lax.ppermute(lax.slice_in_dim(block, block.shape[dim] - width, None, axis...]
    concatenate x15 -> x0, other arithmetic: 14.1 us -> none  [padded_2(): block = jnp.concatenate([low, block, high], axis=dim)]
  transfers between devices with their start and end apart: 31 -> 0, of which waited for: 15 -> 0; matrix products, arithmetic and copies ran while one was open for 4% -> 0% of each run, Pallas kernels for 0% -> 0%
where the time goes in v2:
time: 52.8 us; the launch traced here: 52.6 us
  Pallas kernels  49.3 us (93%)
  local copies, waits for them, and re-layouts  3.18 us (6%)
    pallas_call x1, Pallas kernels, per_device_whole(): pl.pallas_call(whole_kernel, out_shape=jax.ShapeDtypeStruct((rows, half),...  49.3 us
    unnamed x11, local copies, waits for them, and re-layouts  3.18 us

profile of v2, /device:TPU:1, one launch (start us, length us, event | category | flops | bytes accessed | tf_op | source)
XLA Modules:
  0.0 52.6 jit_solution(5206816757469174045)
XLA Ops:
  0.1 0.0 copy-start.2
  0.1 0.0 copy-start.3
  0.1 0.0 copy-start.4
  0.1 0.1 pad_maximum_fusion.scales
  0.2 0.6 %copy-done.2 = s32[64]{0:T(128)S(1)} copy-done((s32[64]{0:T(128)S(1)}, s32[64]{0:T(128)}, u32[]{:S(2)}) %copy-start.2) | copy-done | bytes 280
  0.7 0.0 copy-done.3
  0.7 0.0 copy-done.4
  0.7 0.0 copy-start
  0.7 1.1 %copy-done = f32[6,2,8,2048]{3,2,1,0:T(8,128)S(1)} copy-done((f32[6,2,8,2048]{3,2,1,0:T(8,128)S(1)}, f32[6,2,8,2048]{3,2,1,0:T(8,128)}, u32[]{:S(2)}) %copy-start) | copy-done | bytes 786456
  1.9 0.0 copy-start.1
  1.9 0.8 %copy-done.1 = f32[8,2048]{1,0:T(8,128)S(1)} copy-done((f32[8,2048]{1,0:T(8,128)S(1)}, f32[8,2048]{1,0:T(8,128)}, u32[]{:S(2)}) %copy-start.1) | copy-done | bytes 65560
  2.7 49.3 %solve_wave.1 = f32[8,1024]{1,0:T(8,128)S(1)} custom-call(s32[64]{0:T(128)S(1)} %copy-done.2, s32[2]{0:T(128)S(1)} %copy-done.3, f32[64]{0:T(128)S(1)} %copy-done.4, f32[2]{0:T(128)S(1)} %pad_maximum_fusion.scales, f32[6,2,8,2048]{3,2,1,0:T(8,128)S(1)} %copy-done, f32[8,2048]{1,0:T(8,128)S(1)} %copy-done.1), custom_call_target="tpu_custom_call" | custom-call | tf_op jit(solution)/shard_map/solve_wave/pallas_call | solution.py:505
  52.0 0.6 %copy.7 = f32[8,1024]{1,0:T(8,128)} copy(f32[8,1024]{1,0:T(8,128)S(1)} %solve_wave.1) | data formatting | bytes 65536
Async XLA Ops:
  0.1 0.7 %copy-start.2 = (s32[64]{0:T(128)S(1)}, s32[64]{0:T(128)}, u32[]{:S(2)}) copy-start(s32[64]{0:T(128)} %nodes.1) | copy-start | bytes 772
  0.1 0.7 %copy-start.3 = (s32[2]{0:T(128)S(1)}, s32[2]{0:T(128)}, u32[]{:S(2)}) copy-start(s32[2]{0:T(128)} %pair.1) | copy-start | bytes 28
  0.1 0.7 %copy-start.4 = (f32[64]{0:T(128)S(1)}, f32[64]{0:T(128)}, u32[]{:S(2)}) copy-start(f32[64]{0:T(128)} %gains.1) | copy-start | bytes 772
  0.7 1.1 %copy-start = (f32[6,2,8,2048]{3,2,1,0:T(8,128)S(1)}, f32[6,2,8,2048]{3,2,1,0:T(8,128)}, u32[]{:S(2)}) copy-start(f32[6,2,8,2048]{3,2,1,0:T(8,128)} %prior.1) | copy-start | bytes 2359300
  1.9 0.8 %copy-start.1 = (f32[8,2048]{1,0:T(8,128)S(1)}, f32[8,2048]{1,0:T(8,128)}, u32[]{:S(2)}) copy-start(f32[8,2048]{1,0:T(8,128)} %sigma.1) | copy-start | bytes 196612

commit v3 on v2

--- a/solution.py
+++ b/solution.py
@@ -137,7 +137,7 @@
 PAD = 8
 ROWS = 64
 FIRST = 1
-STEP = 128
+STEP = 256
 
 
 def gathers_whole(shape, electrodes):
@@ -148,15 +148,14 @@
         and rows * strips == ROWS
         and rows == PAD
         and strips >= waves + FIRST
-        and cells % (2 * STEP) == 0
-        and cells // 2 >= 4 * STEP
+        and cells == 2 * PAD * LANES
         and electrodes <= LANES
     )
 
 
 def whole_kernel(
     nodes, pair, gains, scales, prior, sigma, out,
-    fields, section, x, past, q, w, s, diag, up, left, charge, steps, grad, other, mine, parts,
+    fields, section, x, past, r, q, w, s, diag, up, left, charge, source, steps, grad, other, mine, parts,
     sigma_sent, sigma_got, field_sent, field_got, own_sem, core_sent, core_got, sent, got,
 ):
     strips = lax.axis_size("strip")
@@ -239,7 +238,6 @@
 
     each_other(lambda place: sigma_copy(place).start())
     each_other(lambda place: field_copy(place, 0).start())
-
     @pl.when(solver)
     def _():
         own_sigma().start()
@@ -255,15 +253,31 @@
     weight = scales[1]
     lane = lax.broadcasted_iota(jnp.int32, (PAD, LANES), 1)
     second = lane >= ROWS
+    band = lax.broadcasted_iota(jnp.int32, (PAD, LANES), 0)
 
     def swap(block):
         return pltpu.roll(block, ROWS, 1)
 
     def edges(ref):
-        last = ref[pl.ds(half, PAD), :]
-        ref[pl.ds(0, PAD), :] = jnp.where(second, swap(last), 0.0)
-        first = ref[pl.ds(PAD, PAD), :]
-        ref[pl.ds(half + PAD, PAD), :] = jnp.where(second, 0.0, swap(first))
+        last = pltpu.roll(ref[pl.ds(half, PAD), :], 1, 0)
+        ref[pl.ds(0, PAD), :] = jnp.where(
+            band == 0, jnp.where(second, swap(last), 0.0), last
+        )
+        first = pltpu.roll(ref[pl.ds(PAD, PAD), :], PAD - 1, 0)
+        ref[pl.ds(half + PAD, PAD), :] = jnp.where(
+            band == PAD - 1, jnp.where(second, 0.0, swap(first)), first
+        )
+
+    def window(ref, block, shifts):
+        tall = ref[pl.ds(block * STEP, STEP + (shifts - 1) * PAD), :]
+        return [tall[shift * PAD : shift * PAD + STEP] for shift in range(shifts)]
+
+    def turned(ref, read):
+        for b in range(PAD):
+            cols = pl.ds(b * LANES, LANES)
+            more = pl.ds(half + b * LANES, LANES)
+            both = jnp.concatenate([read(0, cols), read(1, more)], 0)
+            ref[pl.ds(PAD + b, LANES, stride=PAD), :] = both.T
 
     def rows(block, shift=0):
         return pl.ds(block * STEP + shift, STEP)
@@ -286,7 +300,9 @@
             sign = jnp.where(pair[0] == e, 1.0, 0.0) - jnp.where(pair[1] == e, 1.0, 0.0)
             charge[0, pl.ds(e, 1), :] = jnp.where(hit, sign, 0.0)
             charge[1, pl.ds(e, 1), :] = jnp.where(hit, gains[e], 0.0)
-            return jnp.where(line == e, lax.rem(col, half), spots)
+            cell = lax.rem(col, half)
+            spot = lax.rem(cell, LANES) * PAD + lax.div(cell, LANES)
+            return jnp.where(line == e, spot, spots)
 
         return lax.fori_loop(0, nodes.shape[0], mark, jnp.full((1, LANES), -1, jnp.int32))
 
@@ -294,55 +310,56 @@
         row_lane = lax.rem(lax.broadcasted_iota(jnp.int32, (STEP, LANES), 1), ROWS)
         top = row_lane == 0
         bottom = row_lane == ROWS - 1
-        for b in range(blocks):
-            cols = pl.ds(b * STEP, STEP)
-            s[rows(b, PAD), :] = jnp.concatenate([section[0, :, cols], section[1, :, cols]], 0).T
+        turned(s, lambda side, cols: section[side, :, pl.ds(cols.start - side * half, LANES)])
         edges(s)
         for b in range(blocks):
-            mid = s[rows(b, PAD), :]
-            face_left = 0.5 * (mid + s[rows(b, PAD - 1), :])
-            face_right = 0.5 * (mid + s[rows(b, PAD + 1), :])
+            before, mid, after = window(s, b, 3)
+            face_left = 0.5 * (mid + before)
+            face_right = 0.5 * (mid + after)
             up[rows(b), :] = jnp.where(top, 0.0, 0.5 * (mid + pltpu.roll(mid, 1, 1)))
             left[rows(b), :] = face_left
             floor = jnp.where(bottom, 0.5 * mid, 0.0)
             diag[rows(b), :] = face_left + face_right + floor + square * mid
         tail = s[pl.ds(half + PAD, PAD), :]
-        left[pl.ds(half, PAD), :] = 0.5 * (tail + s[pl.ds(half + PAD - 1, PAD), :])
+        left[pl.ds(half, PAD), :] = 0.5 * (tail + s[pl.ds(half, PAD), :])
 
     def applied(ref, b):
-        mid = ref[rows(b, PAD), :]
+        before, mid, after = window(ref, b, 3)
+        face_left, face_right = window(left, b, 2)
         flux = up[rows(b), :] * (mid - pltpu.roll(mid, 1, 1))
         result = diag[rows(b), :] * mid + (flux - pltpu.roll(flux, LANES - 1, 1))
-        result = result - left[rows(b), :] * ref[rows(b, PAD - 1), :]
-        return mid, result - left[rows(b, 1), :] * ref[rows(b, PAD + 1), :]
-
-    def solve(c, spots):
+        return mid, result - face_left * before - face_right * after
+
+    def sources(spots):
+        for c in range(2):
+            for b in range(blocks):
+                cell = b * STEP + lax.broadcasted_iota(jnp.int32, (STEP, LANES), 0)
+                source[c, rows(b), :] = jnp.dot(
+                    jnp.where(cell == spots, 1.0, 0.0),
+                    charge[c],
+                    precision=lax.Precision.HIGHEST,
+                    preferred_element_type=jnp.float32,
+                )
+
+    def solve(c):
         xc = x.at[c]
-        for b in range(blocks):
-            one = fields[c, :, pl.ds(b * STEP, STEP)]
-            two = fields[c, :, pl.ds(half + b * STEP, STEP)]
-            xc[rows(b, PAD), :] = jnp.concatenate([one, two], 0).T
+        turned(xc, lambda _, cols: fields[c, :, cols])
         edges(xc)
         for b in range(blocks):
-            cell = b * STEP + lax.broadcasted_iota(jnp.int32, (STEP, LANES), 0)
-            source = jnp.dot(
-                jnp.where(cell == spots, 1.0, 0.0),
-                charge[c],
-                precision=lax.Precision.HIGHEST,
-                preferred_element_type=jnp.float32,
-            )
-            past[0, rows(b, PAD), :] = source - applied(xc, b)[1]
-        edges(past.at[0])
-
-        def image(ref, b, sums):
-            mid, value = applied(ref, b)
+            value = source[c, rows(b), :] - applied(xc, b)[1]
+            r[rows(b, PAD), :] = value
+            past[0, rows(b), :] = value
+        edges(r)
+
+        def image(b, sums):
+            mid, value = applied(r, b)
             w[rows(b), :] = value
             return sums[0] + fold(mid * mid), sums[1] + fold(mid * value)
 
         none = (jnp.zeros((PAD, LANES), jnp.float32),) * 2
         sums = none
         for b in range(blocks):
-            sums = image(past.at[0], b, sums)
+            sums = image(b, sums)
         norm, product = total(sums[0]), total(sums[1])
         size = norm / product
         for b in range(blocks):
@@ -355,25 +372,26 @@
 
         def iterate(k, carry):
             norm, size, ratio = carry
-            now = past.at[k]
-            new = past.at[k + 1]
+            per_norm, per_size = 1.0 / norm, 1.0 / size
 
             def advance(b):
                 along = w[rows(b), :] + ratio * q[rows(b), :]
                 q[rows(b), :] = along
-                new[rows(b, PAD), :] = now[rows(b, PAD), :] - size * along
+                value = r[rows(b, PAD), :] - size * along
+                r[rows(b, PAD), :] = value
+                past[k + 1, rows(b), :] = value
 
             advance(blocks - 1)
             advance(0)
-            edges(new)
+            edges(r)
             sums = none
             for b in range(blocks):
                 if b + 1 < blocks - 1:
                     advance(b + 1)
-                sums = image(new, b, sums)
+                sums = image(b, sums)
             after, product = total(sums[0]), total(sums[1])
-            ratio = after / norm
-            size = after / (product - ratio * after / size)
+            ratio = after * per_norm
+            size = after / (product - ratio * after * per_size)
             steps[0, pl.ds(k + 1, 1), :] = wide(size)
             steps[1, pl.ds(k + 1, 1), :] = wide(ratio)
             return after, size, ratio
@@ -387,7 +405,7 @@
         for b in range(blocks):
             value = xc[rows(b, PAD), :]
             for k in range(ITERS):
-                value = value + shares[k] * past[k, rows(b, PAD), :]
+                value = value + shares[k] * past[k, rows(b), :]
             xc[rows(b, PAD), :] = value
         edges(xc)
 
@@ -415,7 +433,7 @@
 
     @pl.when(solver)
     def _():
-        spots = charges()
+        sources(charges())
         own_sigma().wait()
         from_others(
             lambda source: await_block(
@@ -424,6 +442,7 @@
         )
         core_swap.start()
         core_swap.wait()
+        send_second()
         coefficients()
         own_field(0).wait()
         from_others(
@@ -431,28 +450,29 @@
                 fields.at[0, pl.ds(source * depth, depth), :], field_got.at[0, source]
             )
         )
-        send_second()
-        solve(0, spots)
+        solve(0)
         own_field(1).wait()
         from_others(
             lambda source: await_block(
                 fields.at[1, pl.ds(source * depth, depth), :], field_got.at[1, source]
             )
         )
-        solve(1, spots)
+        solve(1)
 
         row_lane = lax.rem(lax.broadcasted_iota(jnp.int32, (STEP, LANES), 1), ROWS)
         for b in range(blocks):
-            u = x[0, rows(b, PAD), :]
-            v = x[1, rows(b, PAD), :]
+            u_before, u, u_after = window(x.at[0], b, 3)
+            v_before, v, v_after = window(x.at[1], b, 3)
             both = u * v
-            term = (u - x[0, rows(b, PAD - 1), :]) * (v - x[1, rows(b, PAD - 1), :])
-            term = term + (u - x[0, rows(b, PAD + 1), :]) * (v - x[1, rows(b, PAD + 1), :])
+            term = (u - u_before) * (v - v_before)
+            term = term + (u - u_after) * (v - v_after)
             rise = (u - pltpu.roll(u, 1, 1)) * (v - pltpu.roll(v, 1, 1))
             term = term + jnp.where(row_lane == 0, 0.0, rise)
             fall = pltpu.roll(rise, LANES - 1, 1)
             term = term + jnp.where(row_lane == ROWS - 1, both, fall)
-            grad[:, pl.ds(b * STEP, STEP)] = ((-weight) * (square * both + 0.5 * term)).T
+            w[rows(b), :] = (-weight) * (square * both + 0.5 * term)
+        for b in range(PAD):
+            grad[:, pl.ds(b * LANES, LANES)] = w[pl.ds(b, LANES, stride=PAD), :].T
 
         grad_swap.start()
         grad_swap.wait_recv()
@@ -495,7 +515,7 @@
     padded = half + 2 * PAD
     vmem = pl.BlockSpec(memory_space=pltpu.VMEM)
     smem = pl.BlockSpec(memory_space=pltpu.SMEM)
-    anywhere = pl.BlockSpec(memory_space=pl.ANY)
+    anywhere = pl.BlockSpec(memory_space=pltpu.HBM)
     f32 = jnp.float32
     dma = pltpu.SemaphoreType.DMA
 
@@ -511,7 +531,8 @@
             pltpu.VMEM((2, ROWS, cells), f32),
             pltpu.VMEM((2, ROWS, half), f32),
             pltpu.VMEM((2, padded, LANES), f32),
-            pltpu.VMEM((ITERS, padded, LANES), f32),
+            pltpu.VMEM((ITERS, half, LANES), f32),
+            pltpu.VMEM((padded, LANES), f32),
             pltpu.VMEM((half, LANES), f32),
             pltpu.VMEM((half, LANES), f32),
             pltpu.VMEM((padded, LANES), f32),
@@ -519,6 +540,7 @@
             pltpu.VMEM((half, LANES), f32),
             pltpu.VMEM((half + PAD, LANES), f32),
             pltpu.VMEM((2, LANES, LANES), f32),
+            pltpu.VMEM((2, half, LANES), f32),
             pltpu.VMEM((2, 2 * PAD, LANES), f32),
             pltpu.VMEM((LANES, half), f32),
             pltpu.VMEM((ROWS, half), f32),
@@ -535,7 +557,7 @@
             dma((waves,)),
         ],
         compiler_params=pltpu.CompilerParams(
-            collective_id=0, has_side_effects=True, vmem_limit_bytes=40 * 2**20
+            collective_id=0, has_side_effects=True, vmem_limit_bytes=63 * 2**20
         ),
         name="solve_wave",
     )(electrode_nodes, source_pair, innovation, scales, prior_fields, conductivity)

time: 52.8 us -> 50.4 us (0.955)
  local copies, waits for them, and re-layouts: 3.18 us -> 1.38 us
  Pallas kernels: 49.3 us -> 47.8 us
  other arithmetic: 0.08 us -> 0.61 us
    unnamed x11 -> x1, local copies, waits for them, and re-layouts: 3.18 us -> 1.38 us
    pallas_call x1, Pallas kernels: 49.3 us -> 47.8 us  [per_device_whole(): pl.pallas_call(whole_kernel, out_shape=jax.ShapeDtypeStruct((rows, half),...]
    another operation x1, other arithmetic: 0.08 us -> 0.61 us  [per_device_whole(): scales = jnp.stack([wavenum * wavenum, weights])]
where the time goes in v3:
time: 50.4 us; the launch traced here: 49.8 us
  Pallas kernels  47.8 us (95%)
  local copies, waits for them, and re-layouts  1.38 us (3%)
  other arithmetic  0.61 us (1%)
    pallas_call x1, Pallas kernels, per_device_whole(): pl.pallas_call(whole_kernel, out_shape=jax.ShapeDtypeStruct((rows, half),...  47.8 us
    unnamed x1, local copies, waits for them, and re-layouts  1.38 us

profile of v3, /device:TPU:1, one launch (start us, length us, event | category | flops | bytes accessed | tf_op | source)
XLA Modules:
  0.0 49.8 jit_solution(13467218638419281089)
XLA Ops:
  0.1 0.6 %pad_maximum_fusion.scales = f32[2]{0:T(128)} fusion(f32[1]{0:T(128)} %bitcast.1, f32[1]{0:T(128)} %bitcast), kind=kLoop, calls=%fused_computation | loop fusion | flops 2 | bytes 16 | tf_op jit(solution)/shard_map/stack | solution.py:524
  0.7 47.8 %solve_wave.1 = f32[8,1024]{1,0:T(8,128)} custom-call(s32[64]{0:T(128)} %nodes.1, s32[2]{0:T(128)} %pair.1, f32[64]{0:T(128)} %gains.1, f32[2]{0:T(128)} %pad_maximum_fusion.scales, f32[6,2,8,2048]{3,2,1,0:T(8,128)} %prior.1, f32[8,2048]{1,0:T(8,128)} %sigma.1), custom_call_target="tpu_custom_call" | custom-call | tf_op jit(solution)/shard_map/solve_wave/pallas_call | solution.py:525
  48.5 1.4 %copy.7 = f32[8,1024]{1,0:T(8,128)} copy(f32[8,1024]{1,0:T(8,128)} %solve_wave.1) | data formatting | bytes 65536

commit v4 on v3

--- a/solution.py
+++ b/solution.py
@@ -155,7 +155,7 @@
 
 def whole_kernel(
     nodes, pair, gains, scales, prior, sigma, out,
-    fields, section, x, past, r, q, w, s, diag, up, left, charge, source, steps, grad, other, mine, parts,
+    fields, section, x, past, r, q, w, s, diag, up, down, left, charge, source, steps, grad, other, mine, parts,
     sigma_sent, sigma_got, field_sent, field_got, own_sem, core_sent, core_got, sent, got,
 ):
     strips = lax.axis_size("strip")
@@ -316,18 +316,21 @@
             before, mid, after = window(s, b, 3)
             face_left = 0.5 * (mid + before)
             face_right = 0.5 * (mid + after)
-            up[rows(b), :] = jnp.where(top, 0.0, 0.5 * (mid + pltpu.roll(mid, 1, 1)))
+            face_up = jnp.where(top, 0.0, 0.5 * (mid + pltpu.roll(mid, 1, 1)))
+            below = jnp.where(bottom, 0.0, pltpu.roll(mid, LANES - 1, 1))
+            face_down = 0.5 * (mid + below)
+            up[rows(b), :] = face_up
+            down[rows(b), :] = jnp.where(bottom, 0.0, face_down)
             left[rows(b), :] = face_left
-            floor = jnp.where(bottom, 0.5 * mid, 0.0)
-            diag[rows(b), :] = face_left + face_right + floor + square * mid
+            diag[rows(b), :] = face_up + face_down + face_left + face_right + square * mid
         tail = s[pl.ds(half + PAD, PAD), :]
         left[pl.ds(half, PAD), :] = 0.5 * (tail + s[pl.ds(half, PAD), :])
 
     def applied(ref, b):
         before, mid, after = window(ref, b, 3)
         face_left, face_right = window(left, b, 2)
-        flux = up[rows(b), :] * (mid - pltpu.roll(mid, 1, 1))
-        result = diag[rows(b), :] * mid + (flux - pltpu.roll(flux, LANES - 1, 1))
+        result = diag[rows(b), :] * mid - up[rows(b), :] * pltpu.roll(mid, 1, 1)
+        result = result - down[rows(b), :] * pltpu.roll(mid, LANES - 1, 1)
         return mid, result - face_left * before - face_right * after
 
     def sources(spots):
@@ -536,6 +539,7 @@
             pltpu.VMEM((half, LANES), f32),
             pltpu.VMEM((half, LANES), f32),
             pltpu.VMEM((padded, LANES), f32),
+            pltpu.VMEM((half, LANES), f32),
             pltpu.VMEM((half, LANES), f32),
             pltpu.VMEM((half, LANES), f32),
             pltpu.VMEM((half + PAD, LANES), f32),

time: 50.4 us -> 48.7 us (0.966)
  Pallas kernels: 47.8 us -> 46.1 us
    pallas_call x1, Pallas kernels: 47.8 us -> 46.1 us  [per_device_whole(): pl.pallas_call(whole_kernel, out_shape=jax.ShapeDtypeStruct((rows, half),...]
where the time goes in v4:
time: 48.7 us; the launch traced here: 48.1 us
  Pallas kernels  46.1 us (95%)
  local copies, waits for them, and re-layouts  1.38 us (3%)
  other arithmetic  0.61 us (1%)
    pallas_call x1, Pallas kernels, per_device_whole(): pl.pallas_call(whole_kernel, out_shape=jax.ShapeDtypeStruct((rows, half),...  46.1 us
    unnamed x1, local copies, waits for them, and re-layouts  1.38 us

profile of v4, /device:TPU:1, one launch (start us, length us, event | category | flops | bytes accessed | tf_op | source)
XLA Modules:
  0.0 48.1 jit_solution(3543933250603448090)
XLA Ops:
  0.1 0.6 %pad_maximum_fusion.scales = f32[2]{0:T(128)} fusion(f32[1]{0:T(128)} %bitcast.1, f32[1]{0:T(128)} %bitcast), kind=kLoop, calls=%fused_computation | loop fusion | flops 2 | bytes 16 | tf_op jit(solution)/shard_map/stack | solution.py:527
  0.7 46.1 %solve_wave.1 = f32[8,1024]{1,0:T(8,128)} custom-call(s32[64]{0:T(128)} %nodes.1, s32[2]{0:T(128)} %pair.1, f32[64]{0:T(128)} %gains.1, f32[2]{0:T(128)} %pad_maximum_fusion.scales, f32[6,2,8,2048]{3,2,1,0:T(8,128)} %prior.1, f32[8,2048]{1,0:T(8,128)} %sigma.1), custom_call_target="tpu_custom_call" | custom-call | tf_op jit(solution)/shard_map/solve_wave/pallas_call | solution.py:528
  46.7 1.4 %copy.7 = f32[8,1024]{1,0:T(8,128)} copy(f32[8,1024]{1,0:T(8,128)} %solve_wave.1) | data formatting | bytes 65536

commit v5 on v4

--- a/solution.py
+++ b/solution.py
@@ -137,7 +137,7 @@
 PAD = 8
 ROWS = 64
 FIRST = 1
-STEP = 256
+STEP = 512
 
 
 def gathers_whole(shape, electrodes):
@@ -220,7 +220,8 @@
         )
 
     def each_other(body):
-        for place in range(waves):
+        for turn in range(waves):
+            place = lax.rem(strip + turn, waves)
 
             @pl.when(strip != place + FIRST)
             def _(place=place):
@@ -423,7 +424,7 @@
 
     def part_copy(target):
         return remote(
-            mine.at[pl.ds(target * depth, depth), :],
+            mine.at[pl.ds(pl.multiple_of(target * depth, PAD), depth), :],
             parts.at[strip - FIRST],
             sent.at[target],
             got.at[strip - FIRST],
@@ -480,11 +481,8 @@
         grad_swap.start()
         grad_swap.wait_recv()
         mine[...] = grad[pl.ds(pl.multiple_of(core * ROWS, ROWS), ROWS), :] + other[...]
-        for target in range(strips):
-
-            @pl.when(strip != target)
-            def _():
-                part_copy(target).start()
+        for hop in range(1, strips):
+            part_copy(lax.rem(strip + hop, strips)).start()
 
         parts[strip - FIRST] = mine[here, :]
 

time: 48.7 us -> 48.4 us (level)
  no operation moved by 1% of the time
where the time goes in v5:
time: 48.4 us; the launch traced here: 47.8 us
  Pallas kernels  45.8 us (95%)
  local copies, waits for them, and re-layouts  1.38 us (3%)
  other arithmetic  0.61 us (1%)
    pallas_call x1, Pallas kernels, per_device_whole(): pl.pallas_call(whole_kernel, out_shape=jax.ShapeDtypeStruct((rows, half),...  45.8 us
    unnamed x1, local copies, waits for them, and re-layouts  1.38 us

profile of v5, /device:TPU:1, one launch (start us, length us, event | category | flops | bytes accessed | tf_op | source)
XLA Modules:
  0.0 47.8 jit_solution(7286405024339549036)
XLA Ops:
  0.1 0.6 %pad_maximum_fusion.scales = f32[2]{0:T(128)} fusion(f32[1]{0:T(128)} %bitcast.1, f32[1]{0:T(128)} %bitcast), kind=kLoop, calls=%fused_computation | loop fusion | flops 2 | bytes 16 | tf_op jit(solution)/shard_map/stack | solution.py:525
  0.7 45.8 %solve_wave.1 = f32[8,1024]{1,0:T(8,128)} custom-call(s32[64]{0:T(128)} %nodes.1, s32[2]{0:T(128)} %pair.1, f32[64]{0:T(128)} %gains.1, f32[2]{0:T(128)} %pad_maximum_fusion.scales, f32[6,2,8,2048]{3,2,1,0:T(8,128)} %prior.1, f32[8,2048]{1,0:T(8,128)} %sigma.1), custom_call_target="tpu_custom_call" | custom-call | tf_op jit(solution)/shard_map/solve_wave/pallas_call | solution.py:526
  46.5 1.4 %copy.7 = f32[8,1024]{1,0:T(8,128)} copy(f32[8,1024]{1,0:T(8,128)} %solve_wave.1) | data formatting | bytes 65536
